TPU v7x, 128 devices: a whole 4x4x4 slice. The times are simulated.
128 devices in a mesh: group: 16 (over z, x), inner: 8 (over y, core).
Axes of the slice: x: 4, y: 4, z: 4, core: 2. Of those that a mesh axis runs over, the one named last changes fastest.
Arguments:
- density_matrix: bfloat16 [8192, 8192], P('group', 'inner'), may hold values from -0.0029296875 to 0.0029296875
- basis_values: bfloat16 [128, 1536, 2048], P(('group', 'inner')), may hold values from -6 to 6
- block_list: int32 [128, 16], P(('group', 'inner')), may hold values from 0 to 63, as said below
- point_counts: int32 [128], P(('group', 'inner')), may hold values from 1 to 1536, 122880 in all
- core_density: float32 [128, 1536], P(('group', 'inner')), may hold values from 0.5 to 4
- grid_weights: float32 [128, 1536], P(('group', 'inner')), may hold values from 0.0001 to 0.002
Outputs:
- density: float32 [128, 1536], P(('group', 'inner'))
- xc_matrix: float32 [8192, 8192], P('group', 'inner')
Inputs may be any that keep to these rules, and one draw needn't show every extreme that they name: `block_list`: entry i of every batch's list lies in blocks i * 4 to (i + 1) * 4 - 1.
All inputs are finite; a program needn't handle non-finite values. No bound on the sum of `point_counts` on one device may be relied on, other than what follows from the above.
Results may differ from a plain program's by a relative error of at most 0.00095.
Values may be sent and summed in bfloat16 or wider, within the bound.
No kernel may reach another device: no remote copies, remote signals or barrier semaphores. Data moves between devices by JAX's collectives and lax.ppermute only.
A program may use at most 128 MiB of HBM per device.

v0:
```python
import jax
import jax.numpy as jnp
from jax import lax
from jax.experimental import pallas as pl
from jax.experimental.pallas import tpu as pltpu
from jax.sharding import PartitionSpec as P

BLK = 128
KB = 16
GROUPS = 16
INNERS = 8
DEVICES = GROUPS * INNERS
SPAN = 4
SLOT = SPAN * BLK
BUCKETS = SPAN * SPAN
ROWS = BLK + 8
PTS = 1536
COLS = KB * BLK
PAIR = 2 * BLK
AXES = ("group", "inner")

slater_factor = -((3.0 / 3.141592653589793) ** (1.0 / 3.0))
density_floor = 0.1
STEP = float(2**22)
BITS = 14.0
TINY = 2.0**-100
TILE = 512
CHUNK = 512
VMEM_ALL = 60 * 2**20
VMEM_SMALL = 24 * 2**20


def owner(i, j):
    return i * INNERS + j // 2 if (i + j) % 2 == 0 else j * INNERS + i // 2


def chosen_half(g, n):
    odd = g % 2
    return odd if g < 2 * n else 1 - odd


def mirror_pairs():
    pairs = []
    for g in range(GROUPS):
        for n in range(INNERS):
            half = chosen_half(g, n)
            if g // 2 != n:
                half = 1 - half
            pairs.append((g * INNERS + n, (2 * n + half) * INNERS + g // 2))
    return pairs


def row_col(shape):
    return lax.broadcasted_iota(jnp.int32, shape, 0), lax.broadcasted_iota(jnp.int32, shape, 1)


def encode(value):
    return jnp.floor(value * STEP + 0.5).astype(jnp.int32).astype(jnp.int16)


def pick_kernel(flags, index, matrix, mirror, out, table):
    step = pl.program_id(0)
    per_step = out.shape[0]

    @pl.when(step == 0)
    def _():
        flip = flags[0] == 1
        special = flags[1] == 1
        low = flags[2] == 1
        own_start = flags[3] * SLOT
        other_start = SLOT - own_start

        def put(a, b, first, second):
            rows, cols = row_col((BLK, BLK))
            total = first + second.T
            diagonal = jnp.sum(jnp.where(rows == cols, total, 0.0), axis=0, keepdims=True)
            tail = jnp.broadcast_to(diagonal, (ROWS - BLK, BLK))
            table[a * SPAN + b] = encode(jnp.concatenate([total, tail], axis=0))

            @pl.when(special)
            def _():
                at = jnp.where(low, a, b)
                start = pl.multiple_of(at * BLK, BLK)
                side = pl.multiple_of(other_start + at * BLK, BLK)
                block = matrix[pl.ds(start, BLK), pl.ds(side, BLK)].astype(jnp.float32)
                both = jnp.where(rows == cols, block, block + block.T)
                keep = jnp.where(low, rows - cols, cols - rows) > 0
                packed = jnp.where(keep, total, both)
                table[a * SPAN + b] = encode(jnp.concatenate([packed, tail], axis=0))

        def mirror_block(a, b):
            return mirror[a * BLK : (a + 1) * BLK, b * BLK : (b + 1) * BLK].astype(jnp.float32)

        def own_block(a, b):
            start = pl.multiple_of(own_start + b * BLK, BLK)
            return matrix[a * BLK : (a + 1) * BLK, pl.ds(start, BLK)].astype(jnp.float32)

        for a in range(SPAN):
            for b in range(SPAN):

                @pl.when(flip)
                def _():
                    put(a, b, mirror_block(a, b), own_block(b, a))

                @pl.when(jnp.logical_not(flip))
                def _():
                    put(a, b, own_block(a, b), mirror_block(b, a))

    def copy(k, carry):
        out[k] = table[index[step * per_step + k]]
        return carry

    lax.fori_loop(0, per_step, copy, 0, unroll=4)


def pick(flags, index, matrix, mirror):
    per_step = 16
    return pl.pallas_call(
        pick_kernel,
        grid=(DEVICES // per_step,),
        out_shape=jax.ShapeDtypeStruct((DEVICES, ROWS, BLK), jnp.int16),
        in_specs=[
            pl.BlockSpec(memory_space=pltpu.SMEM),
            pl.BlockSpec(memory_space=pltpu.SMEM),
            pl.BlockSpec((SLOT, 2 * SLOT), lambda s: (0, 0)),
            pl.BlockSpec((SLOT, SLOT), lambda s: (0, 0)),
        ],
        out_specs=pl.BlockSpec((per_step, ROWS, BLK), lambda s: (s, 0, 0)),
        scratch_shapes=[pltpu.VMEM((BUCKETS, ROWS, BLK), jnp.int16)],
        compiler_params=pltpu.CompilerParams(vmem_limit_bytes=VMEM_SMALL),
    )(flags, index, matrix, mirror)


def pack(value):
    most = jnp.max(jnp.abs(value), axis=0, keepdims=True)
    power = jnp.ceil(jnp.log2(jnp.maximum(most, TINY)))
    scaled = jnp.floor(value * jnp.exp2(BITS - power) + 0.5).astype(jnp.int32)
    rows, _ = row_col(value.shape)
    return jnp.where(rows > BLK, power.astype(jnp.int32), scaled).astype(jnp.int16)


def unpack(coded):
    wide = coded.astype(jnp.int32).astype(jnp.float32)
    return wide * jnp.exp2(wide[BLK + 1 : BLK + 2] - BITS)


def batch_kernel(
    count,
    blocks_in,
    basis_in,
    turned_in,
    core,
    weights,
    density,
    pieces_out,
    blocks,
    basis,
    turned,
    pieces,
    both,
    total,
    scaled,
    arrived,
    left_here,
):
    def chunk(k):
        at = (slice(None), slice(k * CHUNK, (k + 1) * CHUNK))
        return pltpu.make_async_copy(basis_in.at[at], basis.at[at], arrived.at[k])

    chunks = [chunk(k) for k in range(COLS // CHUNK)]
    load_blocks = pltpu.make_async_copy(blocks_in, blocks, arrived.at[len(chunks)])
    load_turned = pltpu.make_async_copy(turned_in, turned, arrived.at[len(chunks) + 1])
    load_blocks.start()
    chunks[0].start()

    rows, cols = row_col((BLK, BLK))

    def message(device):
        return blocks[device].astype(jnp.int32).astype(jnp.float32)

    def place(side, start, right, value):
        top = value.astype(jnp.bfloat16)
        at = pl.ds(start, BLK)
        both[side, at, right * BLK : (right + 1) * BLK] = top
        rest = (value - top.astype(jnp.float32)).astype(jnp.bfloat16)
        both[side, at, PAIR + right * BLK : PAIR + (right + 1) * BLK] = rest

    def place_pair(big, p):
        for di in range(2):
            for dj in range(2):
                device = (2 * p + di) * INNERS + big if di == dj else (2 * big + dj) * INNERS + p
                start = p * PAIR + di * BLK
                place(big % 2, start, dj, message(device)[:BLK])

    def place_diagonal(big):
        first = message(2 * big * INNERS + big)
        second = message((2 * big + 1) * INNERS + big)
        diagonal = jnp.broadcast_to(first[BLK : BLK + 1], (BLK, BLK))
        first, second = first[:BLK], second[:BLK]
        cross = jnp.where(rows > cols, first, jnp.where(rows < cols, second, diagonal))
        side, start = big % 2, big * PAIR
        place(side, start, 0, jnp.where(rows <= cols, first, 0.0))
        place(side, start, 1, cross)
        place(side, start + BLK, 0, jnp.zeros((BLK, BLK), jnp.float32))
        place(side, start + BLK, 1, jnp.where(rows >= cols, second, 0.0))

    load_blocks.wait()
    place_diagonal(0)
    tiles = PTS // TILE
    for big in range(KB // 2):
        depth = (big + 1) * PAIR
        if big * PAIR % CHUNK == 0:
            k = big * PAIR // CHUNK
            chunks[k].wait()
            if k + 1 < len(chunks):
                chunks[k + 1].start()
            else:
                load_turned.start()

        if big + 1 < KB // 2:
            for p in range(big + 1):
                place_pair(big + 1, p)
        for m in range(tiles):
            at = slice(m * TILE, (m + 1) * TILE)
            product = jnp.dot(
                basis[at, :depth], both[big % 2, :depth], preferred_element_type=jnp.float32
            )
            product = product[:, :PAIR] + product[:, PAIR:]
            product *= basis[at, big * PAIR : (big + 1) * PAIR].astype(jnp.float32)
            folded = product[:, :BLK] + product[:, BLK:]
            total[at] = folded if big == 0 else total[at] + folded
        if big + 1 < KB // 2:
            place_diagonal(big + 1)

    summed = jnp.sum(total[...], axis=1, keepdims=True) * (1.0 / STEP)
    found = core[...] + summed
    density[...] = found
    potential = slater_factor * jnp.exp(jnp.log(jnp.maximum(found, density_floor)) * (1.0 / 3.0))
    live = lax.broadcasted_iota(jnp.int32, (PTS, 1), 0) < count[0]
    total[...] = jnp.broadcast_to(jnp.where(live, weights[...] * potential, 0.0), (PTS, BLK))

    tail = jnp.zeros((ROWS - BLK, BLK), jnp.float32)

    def send(device, value, last=tail):
        pieces[device] = pack(jnp.concatenate([value, last], axis=0))
        pltpu.make_async_copy(pieces.at[device], pieces_out.at[device], left_here).start()

    load_turned.wait()
    for big in range(KB // 2):
        half = big % 2
        for k in range(2):
            lanes = slice(big * PAIR + k * BLK, big * PAIR + (k + 1) * BLK)
            part_of = (total[...] * basis[:, lanes].astype(jnp.float32)).astype(jnp.bfloat16)
            scaled[half, :, k * BLK : (k + 1) * BLK] = part_of
        products = jnp.dot(
            turned[: (big + 1) * PAIR], scaled[half], preferred_element_type=jnp.float32
        )
        for part in range(big + 1):
            product = products[part * PAIR : (part + 1) * PAIR]
            i, j = 2 * part, 2 * big
            if part < big:
                for di in range(2):
                    for dj in range(2):
                        send(
                            owner(i + di, j + dj),
                            product[di * BLK : (di + 1) * BLK, dj * BLK : (dj + 1) * BLK],
                        )
            else:
                cross = product[:BLK, BLK:]
                diagonal = jnp.sum(jnp.where(rows == cols, cross, 0.0), axis=0, keepdims=True)
                last = jnp.broadcast_to(diagonal, (ROWS - BLK, BLK))
                send(i * INNERS + big, jnp.where(rows > cols, cross, product[:BLK, :BLK]), last)
                send((i + 1) * INNERS + big, jnp.where(rows < cols, cross, product[BLK:, BLK:]), last)
    pltpu.make_async_copy(pieces, pieces_out, left_here).wait()


def batch(count, blocks, basis, turned, core, weights):
    vmem = pl.BlockSpec(memory_space=pltpu.VMEM)
    anywhere = pl.BlockSpec(memory_space=pl.ANY)
    messages = (DEVICES, ROWS, BLK)
    return pl.pallas_call(
        batch_kernel,
        out_shape=(
            jax.ShapeDtypeStruct((PTS, 1), jnp.float32),
            jax.ShapeDtypeStruct(messages, jnp.int16),
        ),
        in_specs=[pl.BlockSpec(memory_space=pltpu.SMEM)] + [anywhere] * 3 + [vmem] * 2,
        out_specs=(vmem, pl.BlockSpec(memory_space=pltpu.HBM)),
        scratch_shapes=[
            pltpu.VMEM(messages, jnp.int16),
            pltpu.VMEM((PTS, COLS), jnp.bfloat16),
            pltpu.VMEM((COLS, PTS), jnp.bfloat16),
            pltpu.VMEM(messages, jnp.int16),
            pltpu.VMEM((2, COLS, 2 * PAIR), jnp.bfloat16),
            pltpu.VMEM((PTS, BLK), jnp.float32),
            pltpu.VMEM((2, PTS, PAIR), jnp.bfloat16),
            pltpu.SemaphoreType.DMA((COLS // CHUNK + 2,)),
            pltpu.SemaphoreType.DMA,
        ],
        compiler_params=pltpu.CompilerParams(vmem_limit_bytes=VMEM_ALL),
    )(count, blocks, basis, turned, core, weights)


def sum_kernel(index, pieces, total, copy):
    step = pl.program_id(0)
    per_step = pieces.shape[0]

    @pl.when(step == 0)
    def _():
        total[...] = jnp.zeros_like(total)

    def add(k, carry):
        at = index[step * per_step + k]
        total[at] = total[at] + unpack(pieces[k])
        return carry

    lax.fori_loop(0, per_step, add, 0, unroll=4)

    @pl.when(step == pl.num_programs(0) - 1)
    def _():
        for k in range(BUCKETS):
            copy[k] = pack(total[k])


def sum_pieces(index, pieces):
    per_step = 16
    shape = (BUCKETS, ROWS, BLK)
    whole = pl.BlockSpec(shape, lambda s: (0, 0, 0))
    return pl.pallas_call(
        sum_kernel,
        grid=(DEVICES // per_step,),
        out_shape=(jax.ShapeDtypeStruct(shape, jnp.float32), jax.ShapeDtypeStruct(shape, jnp.int16)),
        in_specs=[
            pl.BlockSpec(memory_space=pltpu.SMEM),
            pl.BlockSpec((per_step, ROWS, BLK), lambda s: (s, 0, 0)),
        ],
        out_specs=(whole, whole),
        compiler_params=pltpu.CompilerParams(vmem_limit_bytes=VMEM_SMALL),
    )(index, pieces)


def finish_kernel(flags, total, mirror, out):
    flip = flags[0] == 1
    special = flags[1] == 1
    half = flags[3]
    rows, cols = row_col((BLK, BLK))

    def slot(which, a, b):
        start = pl.multiple_of(which * SLOT + b * BLK, BLK)
        return (slice(a * BLK, (a + 1) * BLK), pl.ds(start, BLK))

    def received(k):
        return unpack(mirror[k])

    @pl.when(jnp.logical_not(special))
    def _():
        for a in range(SPAN):
            for b in range(SPAN):
                k = a * SPAN + b

                @pl.when(flip)
                def _():
                    out[slot(half, b, a)] = total[k, :BLK].T
                    out[slot(1 - half, b, a)] = received(k)[:BLK].T

                @pl.when(jnp.logical_not(flip))
                def _():
                    out[slot(half, a, b)] = total[k, :BLK]
                    out[slot(1 - half, a, b)] = received(k)[:BLK]

    def diagonal_group(lower):
        for a in range(SPAN):
            for b in range(SPAN):
                k = a * SPAN + b
                mine, theirs = total[k], received(k)
                first, second = (mine, theirs) if lower else (theirs, mine)
                middle = jnp.broadcast_to(first[BLK : BLK + 1], (BLK, BLK))
                cross = jnp.where(
                    rows > cols, first[:BLK], jnp.where(rows < cols, second[:BLK], middle)
                )
                if lower:
                    out[slot(half, a, b)] = cross
                else:
                    out[slot(half, b, a)] = cross.T
                if a != b:
                    out[slot(1 - half, a, b)] = jnp.zeros((BLK, BLK), jnp.float32)
        for a in range(SPAN):
            held = jnp.zeros((BLK, BLK), jnp.float32)
            for b in range(SPAN):
                held += total[a * SPAN + b if lower else b * SPAN + a, :BLK]
            keep = rows < cols if lower else rows > cols
            strict = jnp.where(keep, held, 0.0)
            out[slot(1 - half, a, a)] = jnp.where(rows == cols, held, strict + strict.T)

    @pl.when(jnp.logical_and(special, flags[2] == 1))
    def _():
        diagonal_group(True)

    @pl.when(jnp.logical_and(special, flags[2] == 0))
    def _():
        diagonal_group(False)


def finish(flags, total, mirror):
    vmem = pl.BlockSpec(memory_space=pltpu.VMEM)
    return pl.pallas_call(
        finish_kernel,
        out_shape=jax.ShapeDtypeStruct((SLOT, 2 * SLOT), jnp.float32),
        in_specs=[pl.BlockSpec(memory_space=pltpu.SMEM), vmem, vmem],
        out_specs=vmem,
        compiler_params=pltpu.CompilerParams(vmem_limit_bytes=VMEM_SMALL),
    )(flags, total, mirror)


def per_device(density_matrix, basis_values, block_list, point_counts, core_density, grid_weights):
    g = lax.axis_index("group")
    n = lax.axis_index("inner")
    odd = lax.rem(g, 2)
    half = jnp.where(g < 2 * n, odd, 1 - odd)
    flip = (g > 2 * n).astype(jnp.int32)
    special = g // 2 == n
    column_slot = 2 * n + half
    first, second = jnp.minimum(g, column_slot), jnp.maximum(g, column_slot)
    flags = jnp.stack([flip, special.astype(jnp.int32), 1 - odd, half]).astype(jnp.int32)
    pairs = mirror_pairs()

    basis = basis_values[0]
    left, right = density_matrix[:, :SLOT], density_matrix[:, SLOT:]
    sent = jnp.where((half == 0) == special, left, right)
    mirror = lax.ppermute(sent, AXES, pairs)
    lists = lax.all_to_all(
        jnp.broadcast_to(block_list, (DEVICES, KB)), AXES, split_axis=0, concat_axis=0, tiled=True
    )
    slots = jnp.arange(KB, dtype=jnp.int32)
    factor = jnp.where(slots == first, SPAN, 0) + jnp.where(slots == second, 1, 0)
    index = jnp.sum((lists - slots * SPAN) * factor, axis=1).astype(jnp.int32)

    picked = pick(flags, index, density_matrix, mirror)
    blocks = lax.all_to_all(picked, AXES, split_axis=0, concat_axis=0, tiled=True)
    density, pieces = batch(
        point_counts,
        blocks,
        basis,
        basis.T,
        core_density.reshape(PTS, 1),
        grid_weights.reshape(PTS, 1),
    )
    landed = lax.all_to_all(pieces, AXES, split_axis=0, concat_axis=0, tiled=True)
    total, copy = sum_pieces(index, landed)
    returned = lax.ppermute(copy, AXES, [(target, source) for source, target in pairs])
    return density.reshape(1, PTS), finish(flags, total, returned)


def solution(mesh):
    return jax.shard_map(
        per_device,
        mesh=mesh,
        in_specs=(
            P("group", "inner"),
            P(AXES, None, None),
            P(AXES, None),
            P(AXES),
            P(AXES, None),
            P(AXES, None),
        ),
        out_specs=(P(AXES, None), P("group", "inner")),
        check_vma=False,
    )
```

profile of v0, /device:TPU:96, one launch (start us, length us, event | category | flops | bytes accessed | tf_op | source)
XLA Modules:
  0.0 232.4 jit_solution(11466059712185186891)
XLA Ops:
  0.7 1.3 slice_select_fusion
  1.9 1.7 collective-permute-start
  3.6 1.3 broadcast_in_dim.17
  5.0 9.5 %all-to-all-start = ((s32[128,1,16]{2,1,0:T(1,128)}), s32[128,1,16]{2,1,0:T(1,128)S(1)}, u32[]{:S(2)}, u32[]{:S(2)}) async-start(s32[128,1,16]{2,1,0:T(1,128)} %broadcast_in_dim.17), calls=%async_computation | async-start | bytes 131072 | tf_op jit(solution)/shard_map/all_to_all | solution.py:431
  14.4 0.1 pad_add_fusion.flags
  14.5 19.2 %all-to-all-done = s32[128,1,16]{2,1,0:T(1,128)S(1)} async-done(((s32[128,1,16]{2,1,0:T(1,128)}), s32[128,1,16]{2,1,0:T(1,128)S(1)}, u32[]{:S(2)}, u32[]{:S(2)}) %all-to-all-start) | async-done | bytes 8224 | tf_op jit(solution)/shard_map/all_to_all | solution.py:431
  33.8 0.1 fusion.1.index
  33.9 0.0 collective-permute-done.mirror
  33.9 0.0 copy-start.1
  33.9 1.2 copy-done.1
  35.2 3.1 %shard_map.80 = s16[128,136,128]{2,1,0:T(8,128)(2,1)S(1)} custom-call(s32[4]{0:T(128)S(1)} %pad_add_fusion.flags, s32[128]{0:T(128)S(1)} %fusion.1.index, bf16[512,1024]{1,0:T(8,128)(2,1)S(1)} %copy-done.1, bf16[512,512]{1,0:T(8,128)(2,1)S(1)} %collective-permute-done.mirror), custom_call_target="tpu_custom_call" | custom-call | tf_op jit(solution)/shard_map/pallas_call | solution.py:118
  38.3 0.0 copy-start
  38.3 2.1 copy-done
  40.4 0.0 copy-start.3
  40.4 0.0 copy-start.4
  40.4 7.5 %all-to-all-start.1 = ((s16[128,136,128]{2,1,0:T(8,128)(2,1)}), s16[128,136,128]{2,1,0:T(8,128)(2,1)}, u32[]{:S(2)}, u32[]{:S(2)}) async-start(s16[128,136,128]{2,1,0:T(8,128)(2,1)} %copy-done), calls=%async_computation.1 | async-start | bytes 8912896 | tf_op jit(solution)/shard_map/all_to_all | solution.py:439
  48.6 0.0 copy-done.3
  48.7 1.2 copy.26.core
  49.8 0.0 copy-done.4
  49.8 1.2 copy.27.weights
  51.1 8.6 %copy.24 = bf16[1,1536,2048]{1,2,0:T(8,128)(2,1)} copy(bf16[1,1536,2048]{2,1,0:T(8,128)(2,1)} %param.7) | data formatting | bytes 12582912 | tf_op args[1]
  59.7 41.5 %all-to-all-done.1.blocks_in = s16[128,136,128]{2,1,0:T(8,128)(2,1)} async-done(((s16[128,136,128]{2,1,0:T(8,128)(2,1)}), s16[128,136,128]{2,1,0:T(8,128)(2,1)}, u32[]{:S(2)}, u32[]{:S(2)}) %all-to-all-start.1) | async-done | bytes 4456480 | tf_op jit(solution)/shard_map/all_to_all | solution.py:439
  101.2 33.1 %shard_map.81 = (f32[1536,1]{1,0:T(8,128)}, s16[128,136,128]{2,1,0:T(8,128)(2,1)}) custom-call(s32[1]{0:T(128)S(6)} %copy.29.count, s16[128,136,128]{2,1,0:T(8,128)(2,1)} %all-to-all-done.1.blocks_in, bf16[1536,2048]{1,0:T(8,128)(2,1)} %bitcast.17, bf16[2048,1536]{1,0:T(8,128)(2,1)} %bitcast.18, f32[1536,1]{1,0:T(8,128)} %copy.26.core, f32[1536,1]{1,0:T(8,128)} %copy.27.weights), custom_call_target="tpu_custom_call" | custom-call | tf_op jit(solution)/shard_map/pallas_call | solution.py:281
  134.3 60.9 %all_to_all.19.pieces = s16[128,136,128]{2,1,0:T(8,128)(2,1)S(1)} all-to-all(s16[128,136,128]{2,1,0:T(8,128)(2,1)} %get-tuple-element.7), channel_id=1, replica_groups=mesh['group'=16,'inner'=8] {'group','inner'}, dimensions={0} | all-to-all | bytes 8912896 | tf_op jit(solution)/shard_map/all_to_all | solution.py:448
  195.2 0.0 copy-start.2
  195.2 2.6 %shard_map.82 = (f32[16,136,128]{2,1,0:T(8,128)S(1)}, s16[16,136,128]{2,1,0:T(8,128)(2,1)S(1)}) custom-call(s32[128]{0:T(128)S(1)} %fusion.1.index, s16[128,136,128]{2,1,0:T(8,128)(2,1)S(1)} %all_to_all.19.pieces), custom_call_target="tpu_custom_call" | custom-call | tf_op jit(solution)/shard_map/pallas_call | solution.py:329
  197.9 3.1 %collective-permute-start.1 = (s16[16,136,128]{2,1,0:T(8,128)(2,1)S(1)}, s16[16,136,128]{2,1,0:T(8,128)(2,1)S(1)}, u32[]{:S(2)}, u32[]{:S(2)}) collective-permute-start(s16[16,136,128]{2,1,0:T(8,128)(2,1)S(1)} %get-tuple-element.9), channel_id=1, source_target_pairs={{8,0},{24,1},{40,2},{56,3},{72,4},{88,5},{104,6},{120,7},{0,8},{16... | collective-permute-start | bytes 1671176 | tf_op jit(solution)/shard_map/ppermute | solution.py:450
  201.0 0.0 copy-done.2
  201.0 0.3 reduce
  201.3 0.6 reshape.34
  201.9 26.8 %collective-permute-done.1.mirror = s16[16,136,128]{2,1,0:T(8,128)(2,1)S(1)} collective-permute-done((s16[16,136,128]{2,1,0:T(8,128)(2,1)S(1)}, s16[16,136,128]{2,1,0:T(8,128)(2,1)S(1)}, u32[]{:S(2)}, u32[]{:S(2)}) %collective-permute-start.1) | collective-permute-done | bytes 557088 | tf_op jit(solution)/shard_map/ppermute | solution.py:450
  228.7 3.7 %shard_map.83 = f32[512,1024]{1,0:T(8,128)} custom-call(s32[4]{0:T(128)S(1)} %pad_add_fusion.flags, f32[16,136,128]{2,1,0:T(8,128)S(1)} %get-tuple-element.8.total, s16[16,136,128]{2,1,0:T(8,128)(2,1)S(1)} %collective-permute-done.1.mirror), custom_call_target="tpu_custom_call" | custom-call | tf_op jit(solution)/shard_map/pallas_call | solution.py:406
  (2 shorter events, 0.1 us)
Async XLA Ops:
  1.9 32.0 %collective-permute-start = (bf16[512,512]{1,0:T(8,128)(2,1)S(1)}, bf16[512,512]{1,0:T(8,128)(2,1)S(1)}, u32[]{:S(2)}, u32[]{:S(2)}) collective-permute-start(bf16[512,512]{1,0:T(8,128)(2,1)S(1)} %slice_select_fusion), channel_id=1, source_target_pairs={{0,8},{1,24},{2,40},{3,56},{4,72},{5,88},{6,104},{7,120},{8,0},{9,... | collective-permute-start | bytes 1572872 | tf_op jit(solution)/shard_map/ppermute | solution.py:430
  5.0 28.8 %all-to-all-start = ((s32[128,1,16]{2,1,0:T(1,128)}), s32[128,1,16]{2,1,0:T(1,128)S(1)}, u32[]{:S(2)}, u32[]{:S(2)}) async-start(s32[128,1,16]{2,1,0:T(1,128)} %broadcast_in_dim.17), calls=%async_computation | async-start | bytes 131072 | tf_op jit(solution)/shard_map/all_to_all | solution.py:431
  33.9 1.2 copy-start.1
  38.3 2.2 copy-start
  40.4 8.2 %copy-start.3 = (f32[1,1536]{1,0:T(1,128)S(1)}, f32[1,1536]{1,0:T(1,128)}, u32[]{:S(2)}) copy-start(f32[1,1536]{1,0:T(1,128)} %param.10) | copy-start | bytes 18436
  40.4 9.4 %copy-start.4 = (f32[1,1536]{1,0:T(1,128)S(1)}, f32[1,1536]{1,0:T(1,128)}, u32[]{:S(2)}) copy-start(f32[1,1536]{1,0:T(1,128)} %param.11) | copy-start | bytes 18436
  40.4 60.7 %all-to-all-start.1 = ((s16[128,136,128]{2,1,0:T(8,128)(2,1)}), s16[128,136,128]{2,1,0:T(8,128)(2,1)}, u32[]{:S(2)}, u32[]{:S(2)}) async-start(s16[128,136,128]{2,1,0:T(8,128)(2,1)} %copy-done), calls=%async_computation.1 | async-start | bytes 8912896 | tf_op jit(solution)/shard_map/all_to_all | solution.py:439
  195.2 5.8 %copy-start.2 = (f32[1536,1]{1,0:T(8,128)S(1)}, f32[1536,1]{1,0:T(8,128)}, u32[]{:S(2)}) copy-start(f32[1536,1]{1,0:T(8,128)} %get-tuple-element.6) | copy-start | bytes 18436
  197.9 30.8 %collective-permute-start.1 = (s16[16,136,128]{2,1,0:T(8,128)(2,1)S(1)}, s16[16,136,128]{2,1,0:T(8,128)(2,1)S(1)}, u32[]{:S(2)}, u32[]{:S(2)}) collective-permute-start(s16[16,136,128]{2,1,0:T(8,128)(2,1)S(1)} %get-tuple-element.9), channel_id=1, source_target_pairs={{8,0},{24,1},{40,2},{56,3},{72,4},{88,5},{104,6},{120,7},{0,8},{16... | collective-permute-start | bytes 1671176 | tf_op jit(solution)/shard_map/ppermute | solution.py:450
where the time goes:
time: 233 us; the launch traced here: 232 us
  waiting for transfers between devices  87.6 us (38%)
  blocking collectives  60.9 us (26%)
  Pallas kernels  42.5 us (18%)
  starting transfers between devices  21.8 us (9%)
  local copies, waits for them, and re-layouts  16.4 us (7%)
    all_to_all x1, blocking collectives, per_device(): lax.all_to_all(pieces, AXES, split_axis=0, concat_axis=0, tiled=True)  60.9 us
    all_to_all x1, waiting for transfers between devices, per_device(): lax.all_to_all(picked, AXES, split_axis=0, concat_axis=0, tiled=True)  41.5 us
    pallas_call x1, Pallas kernels, batch(): pl.pallas_call(batch_kernel, out_shape=(jax.ShapeDtypeStruct((PTS, 1), jn...  33.1 us
    ppermute x1, waiting for transfers between devices, per_device(): lax.ppermute(copy, AXES, [(target, source) for source, target in pairs])  26.8 us
    all_to_all x1, waiting for transfers between devices, per_device(): lax.all_to_all(jnp.broadcast_to(block_list, (DEVICES, KB)), AXES, split_a...  19.2 us
    unnamed x11, local copies, waits for them, and re-layouts  12 us
    all_to_all x1, starting transfers between devices, per_device(): lax.all_to_all(jnp.broadcast_to(block_list, (DEVICES, KB)), AXES, split_a...  9.46 us
    all_to_all x1, starting transfers between devices, per_device(): lax.all_to_all(picked, AXES, split_axis=0, concat_axis=0, tiled=True)  7.54 us
  transfers between devices with their start and end apart: 4, of which 3 were waited for; matrix products, arithmetic and copies ran while one was open for 6% of the time, Pallas kernels for 0%

commit v1 on v0

--- a/solution.py
+++ b/solution.py
@@ -24,7 +24,7 @@
 STEP = float(2**22)
 BITS = 14.0
 TINY = 2.0**-100
-TILE = 512
+TILE = 256
 CHUNK = 512
 VMEM_ALL = 60 * 2**20
 VMEM_SMALL = 24 * 2**20
@@ -148,6 +148,7 @@
     count,
     blocks_in,
     basis_in,
+    coarse_in,
     turned_in,
     core,
     weights,
@@ -155,23 +156,29 @@
     pieces_out,
     blocks,
     basis,
+    coarse,
     turned,
     pieces,
-    both,
+    high,
+    fine,
     total,
     scaled,
     arrived,
     left_here,
 ):
-    def chunk(k):
-        at = (slice(None), slice(k * CHUNK, (k + 1) * CHUNK))
-        return pltpu.make_async_copy(basis_in.at[at], basis.at[at], arrived.at[k])
-
-    chunks = [chunk(k) for k in range(COLS // CHUNK)]
+    def chunk(k, source, target, at):
+        lanes = (slice(None), slice(k * CHUNK, (k + 1) * CHUNK))
+        return pltpu.make_async_copy(source.at[lanes], target.at[lanes], arrived.at[at])
+
+    chunks = []
+    for k in range(COLS // CHUNK):
+        chunks.append(chunk(k, basis_in, basis, 2 * k))
+        chunks.append(chunk(k, coarse_in, coarse, 2 * k + 1))
     load_blocks = pltpu.make_async_copy(blocks_in, blocks, arrived.at[len(chunks)])
     load_turned = pltpu.make_async_copy(turned_in, turned, arrived.at[len(chunks) + 1])
     load_blocks.start()
     chunks[0].start()
+    chunks[1].start()
 
     rows, cols = row_col((BLK, BLK))
 
@@ -181,9 +188,9 @@
     def place(side, start, right, value):
         top = value.astype(jnp.bfloat16)
         at = pl.ds(start, BLK)
-        both[side, at, right * BLK : (right + 1) * BLK] = top
-        rest = (value - top.astype(jnp.float32)).astype(jnp.bfloat16)
-        both[side, at, PAIR + right * BLK : PAIR + (right + 1) * BLK] = rest
+        high[side, at, right * BLK : (right + 1) * BLK] = top
+        rest = (value - top.astype(jnp.float32)).astype(jnp.float8_e4m3fn)
+        fine[side, at, right * BLK : (right + 1) * BLK] = rest
 
     def place_pair(big, p):
         for di in range(2):
@@ -210,22 +217,23 @@
     for big in range(KB // 2):
         depth = (big + 1) * PAIR
         if big * PAIR % CHUNK == 0:
-            k = big * PAIR // CHUNK
+            k = 2 * (big * PAIR // CHUNK)
             chunks[k].wait()
-            if k + 1 < len(chunks):
-                chunks[k + 1].start()
+            chunks[k + 1].wait()
+            if k + 2 < len(chunks):
+                chunks[k + 2].start()
+                chunks[k + 3].start()
             else:
                 load_turned.start()
 
-        if big + 1 < KB // 2:
-            for p in range(big + 1):
-                place_pair(big + 1, p)
         for m in range(tiles):
+            if big + 1 < KB // 2:
+                for p in range(m, big + 1, tiles):
+                    place_pair(big + 1, p)
             at = slice(m * TILE, (m + 1) * TILE)
-            product = jnp.dot(
-                basis[at, :depth], both[big % 2, :depth], preferred_element_type=jnp.float32
-            )
-            product = product[:, :PAIR] + product[:, PAIR:]
+            side = big % 2
+            product = jnp.dot(basis[at, :depth], high[side, :depth], preferred_element_type=jnp.float32)
+            product += jnp.dot(coarse[at, :depth], fine[side, :depth], preferred_element_type=jnp.float32)
             product *= basis[at, big * PAIR : (big + 1) * PAIR].astype(jnp.float32)
             folded = product[:, :BLK] + product[:, BLK:]
             total[at] = folded if big == 0 else total[at] + folded
@@ -245,18 +253,23 @@
         pieces[device] = pack(jnp.concatenate([value, last], axis=0))
         pltpu.make_async_copy(pieces.at[device], pieces_out.at[device], left_here).start()
 
+    def weigh(big, low, high_end):
+        for k in range(2):
+            lanes = slice(big * PAIR + k * BLK, big * PAIR + (k + 1) * BLK)
+            at = slice(low, high_end)
+            part_of = (total[at] * basis[at, lanes].astype(jnp.float32)).astype(jnp.bfloat16)
+            scaled[big % 2, at, k * BLK : (k + 1) * BLK] = part_of
+
+    weigh(0, 0, PTS)
     load_turned.wait()
     for big in range(KB // 2):
-        half = big % 2
-        for k in range(2):
-            lanes = slice(big * PAIR + k * BLK, big * PAIR + (k + 1) * BLK)
-            part_of = (total[...] * basis[:, lanes].astype(jnp.float32)).astype(jnp.bfloat16)
-            scaled[half, :, k * BLK : (k + 1) * BLK] = part_of
-        products = jnp.dot(
-            turned[: (big + 1) * PAIR], scaled[half], preferred_element_type=jnp.float32
-        )
+        cuts = [PTS // 16 * k // (big + 1) * 16 for k in range(big + 2)]
         for part in range(big + 1):
-            product = products[part * PAIR : (part + 1) * PAIR]
+            product = jnp.dot(
+                turned[part * PAIR : (part + 1) * PAIR], scaled[big % 2], preferred_element_type=jnp.float32
+            )
+            if big + 1 < KB // 2:
+                weigh(big + 1, cuts[part], cuts[part + 1])
             i, j = 2 * part, 2 * big
             if part < big:
                 for di in range(2):
@@ -274,7 +287,7 @@
     pltpu.make_async_copy(pieces, pieces_out, left_here).wait()
 
 
-def batch(count, blocks, basis, turned, core, weights):
+def batch(count, blocks, basis, coarse, turned, core, weights):
     vmem = pl.BlockSpec(memory_space=pltpu.VMEM)
     anywhere = pl.BlockSpec(memory_space=pl.ANY)
     messages = (DEVICES, ROWS, BLK)
@@ -284,21 +297,23 @@
             jax.ShapeDtypeStruct((PTS, 1), jnp.float32),
             jax.ShapeDtypeStruct(messages, jnp.int16),
         ),
-        in_specs=[pl.BlockSpec(memory_space=pltpu.SMEM)] + [anywhere] * 3 + [vmem] * 2,
+        in_specs=[pl.BlockSpec(memory_space=pltpu.SMEM)] + [anywhere] * 4 + [vmem] * 2,
         out_specs=(vmem, pl.BlockSpec(memory_space=pltpu.HBM)),
         scratch_shapes=[
             pltpu.VMEM(messages, jnp.int16),
             pltpu.VMEM((PTS, COLS), jnp.bfloat16),
+            pltpu.VMEM((PTS, COLS), jnp.float8_e4m3fn),
             pltpu.VMEM((COLS, PTS), jnp.bfloat16),
             pltpu.VMEM(messages, jnp.int16),
-            pltpu.VMEM((2, COLS, 2 * PAIR), jnp.bfloat16),
+            pltpu.VMEM((2, COLS, PAIR), jnp.bfloat16),
+            pltpu.VMEM((2, COLS, PAIR), jnp.float8_e4m3fn),
             pltpu.VMEM((PTS, BLK), jnp.float32),
             pltpu.VMEM((2, PTS, PAIR), jnp.bfloat16),
-            pltpu.SemaphoreType.DMA((COLS // CHUNK + 2,)),
+            pltpu.SemaphoreType.DMA((2 * (COLS // CHUNK) + 2,)),
             pltpu.SemaphoreType.DMA,
         ],
         compiler_params=pltpu.CompilerParams(vmem_limit_bytes=VMEM_ALL),
-    )(count, blocks, basis, turned, core, weights)
+    )(count, blocks, basis, coarse, turned, core, weights)
 
 
 def sum_kernel(index, pieces, total, copy):
@@ -441,6 +456,7 @@
         point_counts,
         blocks,
         basis,
+        basis.astype(jnp.float8_e4m3fn),
         basis.T,
         core_density.reshape(PTS, 1),
         grid_weights.reshape(PTS, 1),

time: 233 us -> 229 us (0.983)
  waiting for transfers between devices: 87.6 us -> 77.1 us
  local copies, waits for them, and re-layouts: 16.4 us -> 21.9 us
  other arithmetic: 1.71 us -> 6.65 us
  Pallas kernels: 42.5 us -> 38.6 us
    all_to_all x1, waiting for transfers between devices: 41.5 us -> 31 us  [per_device(): lax.all_to_all(picked, AXES, split_axis=0, concat_axis=0, tiled=True)]
    convert_element_type x0 -> x1, local copies, waits for them, and re-layouts: none -> 5.55 us  [per_device(): basis.astype(jnp.float8_e4m3fn)]
    convert_element_type x0 -> x1, other arithmetic: none -> 4.94 us  [per_device(): basis.astype(jnp.float8_e4m3fn)]
    pallas_call x1, Pallas kernels: 33.1 us -> 29.1 us  [batch(): pl.pallas_call(batch_kernel, out_shape=(jax.ShapeDtypeStruct((PTS, 1), jn...]
  transfers between devices with their start and end apart: 4 -> 4, of which waited for: 3 -> 3; matrix products, arithmetic and copies ran while one was open for 6% -> 10% of each run, Pallas kernels for 0% -> 0%
where the time goes in v1:
time: 229 us; the launch traced here: 228 us
  waiting for transfers between devices  77.1 us (34%)
  blocking collectives  60.9 us (27%)
  Pallas kernels  38.6 us (17%)
  local copies, waits for them, and re-layouts  21.9 us (10%)
  starting transfers between devices  21.8 us (10%)
  other arithmetic  6.65 us (3%)
    all_to_all x1, blocking collectives, per_device(): lax.all_to_all(pieces, AXES, split_axis=0, concat_axis=0, tiled=True)  60.9 us
    all_to_all x1, waiting for transfers between devices, per_device(): lax.all_to_all(picked, AXES, split_axis=0, concat_axis=0, tiled=True)  31 us
    pallas_call x1, Pallas kernels, batch(): pl.pallas_call(batch_kernel, out_shape=(jax.ShapeDtypeStruct((PTS, 1), jn...  29.1 us
    ppermute x1, waiting for transfers between devices, per_device(): lax.ppermute(copy, AXES, [(target, source) for source, target in pairs])  26.8 us
    all_to_all x1, waiting for transfers between devices, per_device(): lax.all_to_all(jnp.broadcast_to(block_list, (DEVICES, KB)), AXES, split_a...  19.2 us
    unnamed x11, local copies, waits for them, and re-layouts  12 us
    all_to_all x1, starting transfers between devices, per_device(): lax.all_to_all(jnp.broadcast_to(block_list, (DEVICES, KB)), AXES, split_a...  9.46 us
    all_to_all x1, starting transfers between devices, per_device(): lax.all_to_all(picked, AXES, split_axis=0, concat_axis=0, tiled=True)  7.54 us
  transfers between devices with their start and end apart: 4, of which 3 were waited for; matrix products, arithmetic and copies ran while one was open for 10% of the time, Pallas kernels for 0%

profile of v1, /device:TPU:96, one launch (start us, length us, event | category | flops | bytes accessed | tf_op | source)
XLA Modules:
  0.0 228.4 jit_solution(10886945897751433690)
XLA Ops:
  0.7 1.3 slice_select_fusion
  1.9 1.7 collective-permute-start
  3.6 1.3 broadcast_in_dim.17
  5.0 9.5 %all-to-all-start = ((s32[128,1,16]{2,1,0:T(1,128)}), s32[128,1,16]{2,1,0:T(1,128)S(1)}, u32[]{:S(2)}, u32[]{:S(2)}) async-start(s32[128,1,16]{2,1,0:T(1,128)} %broadcast_in_dim.17), calls=%async_computation | async-start | bytes 131072 | tf_op jit(solution)/shard_map/all_to_all | solution.py:446
  14.4 0.1 pad_add_fusion.flags
  14.5 19.2 %all-to-all-done = s32[128,1,16]{2,1,0:T(1,128)S(1)} async-done(((s32[128,1,16]{2,1,0:T(1,128)}), s32[128,1,16]{2,1,0:T(1,128)S(1)}, u32[]{:S(2)}, u32[]{:S(2)}) %all-to-all-start) | async-done | bytes 8224 | tf_op jit(solution)/shard_map/all_to_all | solution.py:446
  33.8 0.1 fusion.1.index
  33.9 0.0 collective-permute-done.mirror
  33.9 0.0 copy-start.1
  33.9 1.2 copy-done.1
  35.2 3.1 %shard_map.80 = s16[128,136,128]{2,1,0:T(8,128)(2,1)S(1)} custom-call(s32[4]{0:T(128)S(1)} %pad_add_fusion.flags, s32[128]{0:T(128)S(1)} %fusion.1.index, bf16[512,1024]{1,0:T(8,128)(2,1)S(1)} %copy-done.1, bf16[512,512]{1,0:T(8,128)(2,1)S(1)} %collective-permute-done.mirror), custom_call_target="tpu_custom_call" | custom-call | tf_op jit(solution)/shard_map/pallas_call | solution.py:118
  38.3 0.0 copy-start
  38.3 2.1 copy-done
  40.4 0.0 copy-start.3
  40.4 0.0 copy-start.4
  40.4 7.5 %all-to-all-start.1 = ((s16[128,136,128]{2,1,0:T(8,128)(2,1)}), s16[128,136,128]{2,1,0:T(8,128)(2,1)}, u32[]{:S(2)}, u32[]{:S(2)}) async-start(s16[128,136,128]{2,1,0:T(8,128)(2,1)} %copy-done), calls=%async_computation.1 | async-start | bytes 8912896 | tf_op jit(solution)/shard_map/all_to_all | solution.py:454
  48.6 0.0 copy-done.3
  48.7 1.2 copy.31.core
  49.8 0.0 copy-done.4
  49.8 1.2 copy.32.weights
  51.0 8.6 %copy.28 = bf16[1,1536,2048]{1,2,0:T(8,128)(2,1)} copy(bf16[1,1536,2048]{2,1,0:T(8,128)(2,1)} %param.7) | data formatting | bytes 12582912 | tf_op args[1]
  59.7 4.9 %bitcast_convert_fusion = f8e4m3fn[1536,2048]{0,1:T(32,128)(4,1)S(1)} fusion(bf16[1,1536,2048]{1,2,0:T(8,128)(2,1)} %copy.28), kind=kLoop, calls=%fused_computation | loop fusion | flops 3145728 | bytes 9437184 | tf_op jit(solution)/shard_map/convert_element_type | solution.py:459
  64.6 5.6 %copy.30.coarse_in = f8e4m3fn[1536,2048]{1,0:T(32,128)(4,1)} copy(f8e4m3fn[1536,2048]{0,1:T(32,128)(4,1)S(1)} %bitcast_convert_fusion) | data formatting | bytes 6291456 | tf_op jit(solution)/shard_map/convert_element_type | solution.py:459
  70.2 31.0 %all-to-all-done.1.blocks_in = s16[128,136,128]{2,1,0:T(8,128)(2,1)} async-done(((s16[128,136,128]{2,1,0:T(8,128)(2,1)}), s16[128,136,128]{2,1,0:T(8,128)(2,1)}, u32[]{:S(2)}, u32[]{:S(2)}) %all-to-all-start.1) | async-done | bytes 4456480 | tf_op jit(solution)/shard_map/all_to_all | solution.py:454
  101.2 29.1 %shard_map.81 = (f32[1536,1]{1,0:T(8,128)}, s16[128,136,128]{2,1,0:T(8,128)(2,1)}) custom-call(s32[1]{0:T(128)S(6)} %copy.34.count, s16[128,136,128]{2,1,0:T(8,128)(2,1)} %all-to-all-done.1.blocks_in, bf16[1536,2048]{1,0:T(8,128)(2,1)} %bitcast.19, f8e4m3fn[1536,2048]{1,0:T(32,128)(4,1)} %copy.30.coarse_in, bf16[2048,1536]{1,0:T(8,128)(2,1)} %bitcast.18, ...), custom_call_target="tpu_custom_call" | custom-call | tf_op jit(solution)/shard_map/pallas_call | solution.py:294
  130.4 60.9 %all_to_all.19.pieces = s16[128,136,128]{2,1,0:T(8,128)(2,1)S(1)} all-to-all(s16[128,136,128]{2,1,0:T(8,128)(2,1)} %get-tuple-element.7), channel_id=1, replica_groups=mesh['group'=16,'inner'=8] {'group','inner'}, dimensions={0} | all-to-all | bytes 8912896 | tf_op jit(solution)/shard_map/all_to_all | solution.py:464
  191.3 0.0 copy-start.2
  191.3 2.6 %shard_map.82 = (f32[16,136,128]{2,1,0:T(8,128)S(1)}, s16[16,136,128]{2,1,0:T(8,128)(2,1)S(1)}) custom-call(s32[128]{0:T(128)S(1)} %fusion.1.index, s16[128,136,128]{2,1,0:T(8,128)(2,1)S(1)} %all_to_all.19.pieces), custom_call_target="tpu_custom_call" | custom-call | tf_op jit(solution)/shard_map/pallas_call | solution.py:344
  193.9 3.1 %collective-permute-start.1 = (s16[16,136,128]{2,1,0:T(8,128)(2,1)S(1)}, s16[16,136,128]{2,1,0:T(8,128)(2,1)S(1)}, u32[]{:S(2)}, u32[]{:S(2)}) collective-permute-start(s16[16,136,128]{2,1,0:T(8,128)(2,1)S(1)} %get-tuple-element.9), channel_id=1, source_target_pairs={{8,0},{24,1},{40,2},{56,3},{72,4},{88,5},{104,6},{120,7},{0,8},{16... | collective-permute-start | bytes 1671176 | tf_op jit(solution)/shard_map/ppermute | solution.py:466
  197.0 0.0 copy-done.2
  197.0 0.3 reduce
  197.3 0.6 reshape.34
  197.9 26.8 %collective-permute-done.1.mirror = s16[16,136,128]{2,1,0:T(8,128)(2,1)S(1)} collective-permute-done((s16[16,136,128]{2,1,0:T(8,128)(2,1)S(1)}, s16[16,136,128]{2,1,0:T(8,128)(2,1)S(1)}, u32[]{:S(2)}, u32[]{:S(2)}) %collective-permute-start.1) | collective-permute-done | bytes 557088 | tf_op jit(solution)/shard_map/ppermute | solution.py:466
  224.8 3.7 %shard_map.83 = f32[512,1024]{1,0:T(8,128)} custom-call(s32[4]{0:T(128)S(1)} %pad_add_fusion.flags, f32[16,136,128]{2,1,0:T(8,128)S(1)} %get-tuple-element.8.total, s16[16,136,128]{2,1,0:T(8,128)(2,1)S(1)} %collective-permute-done.1.mirror), custom_call_target="tpu_custom_call" | custom-call | tf_op jit(solution)/shard_map/pallas_call | solution.py:421
  (2 shorter events, 0.1 us)
Async XLA Ops:
  1.9 32.0 %collective-permute-start = (bf16[512,512]{1,0:T(8,128)(2,1)S(1)}, bf16[512,512]{1,0:T(8,128)(2,1)S(1)}, u32[]{:S(2)}, u32[]{:S(2)}) collective-permute-start(bf16[512,512]{1,0:T(8,128)(2,1)S(1)} %slice_select_fusion), channel_id=1, source_target_pairs={{0,8},{1,24},{2,40},{3,56},{4,72},{5,88},{6,104},{7,120},{8,0},{9,... | collective-permute-start | bytes 1572872 | tf_op jit(solution)/shard_map/ppermute | solution.py:445
  5.0 28.8 %all-to-all-start = ((s32[128,1,16]{2,1,0:T(1,128)}), s32[128,1,16]{2,1,0:T(1,128)S(1)}, u32[]{:S(2)}, u32[]{:S(2)}) async-start(s32[128,1,16]{2,1,0:T(1,128)} %broadcast_in_dim.17), calls=%async_computation | async-start | bytes 131072 | tf_op jit(solution)/shard_map/all_to_all | solution.py:446
  33.9 1.2 copy-start.1
  38.3 2.2 copy-start
  40.4 8.2 %copy-start.3 = (f32[1,1536]{1,0:T(1,128)S(1)}, f32[1,1536]{1,0:T(1,128)}, u32[]{:S(2)}) copy-start(f32[1,1536]{1,0:T(1,128)} %param.10) | copy-start | bytes 18436
  40.4 9.4 %copy-start.4 = (f32[1,1536]{1,0:T(1,128)S(1)}, f32[1,1536]{1,0:T(1,128)}, u32[]{:S(2)}) copy-start(f32[1,1536]{1,0:T(1,128)} %param.11) | copy-start | bytes 18436
  40.4 60.7 %all-to-all-start.1 = ((s16[128,136,128]{2,1,0:T(8,128)(2,1)}), s16[128,136,128]{2,1,0:T(8,128)(2,1)}, u32[]{:S(2)}, u32[]{:S(2)}) async-start(s16[128,136,128]{2,1,0:T(8,128)(2,1)} %copy-done), calls=%async_computation.1 | async-start | bytes 8912896 | tf_op jit(solution)/shard_map/all_to_all | solution.py:454
  191.3 5.8 %copy-start.2 = (f32[1536,1]{1,0:T(8,128)S(1)}, f32[1536,1]{1,0:T(8,128)}, u32[]{:S(2)}) copy-start(f32[1536,1]{1,0:T(8,128)} %get-tuple-element.6) | copy-start | bytes 18436
  193.9 30.8 %collective-permute-start.1 = (s16[16,136,128]{2,1,0:T(8,128)(2,1)S(1)}, s16[16,136,128]{2,1,0:T(8,128)(2,1)S(1)}, u32[]{:S(2)}, u32[]{:S(2)}) collective-permute-start(s16[16,136,128]{2,1,0:T(8,128)(2,1)S(1)} %get-tuple-element.9), channel_id=1, source_target_pairs={{8,0},{24,1},{40,2},{56,3},{72,4},{88,5},{104,6},{120,7},{0,8},{16... | collective-permute-start | bytes 1671176 | tf_op jit(solution)/shard_map/ppermute | solution.py:466

commit v2 on v1

--- a/solution.py
+++ b/solution.py
@@ -26,7 +26,7 @@
 TINY = 2.0**-100
 TILE = 256
 CHUNK = 512
-VMEM_ALL = 60 * 2**20
+VMEM_BATCH = 38 * 2**20
 VMEM_SMALL = 24 * 2**20
 
 
@@ -58,7 +58,7 @@
     return jnp.floor(value * STEP + 0.5).astype(jnp.int32).astype(jnp.int16)
 
 
-def pick_kernel(flags, index, matrix, mirror, out, table):
+def pick_kernel(flags, index, own, other, mirror, out, table):
     step = pl.program_id(0)
     per_step = out.shape[0]
 
@@ -67,8 +67,6 @@
         flip = flags[0] == 1
         special = flags[1] == 1
         low = flags[2] == 1
-        own_start = flags[3] * SLOT
-        other_start = SLOT - own_start
 
         def put(a, b, first, second):
             rows, cols = row_col((BLK, BLK))
@@ -81,30 +79,25 @@
             def _():
                 at = jnp.where(low, a, b)
                 start = pl.multiple_of(at * BLK, BLK)
-                side = pl.multiple_of(other_start + at * BLK, BLK)
-                block = matrix[pl.ds(start, BLK), pl.ds(side, BLK)].astype(jnp.float32)
+                block = other[pl.ds(start, BLK), pl.ds(start, BLK)].astype(jnp.float32)
                 both = jnp.where(rows == cols, block, block + block.T)
                 keep = jnp.where(low, rows - cols, cols - rows) > 0
                 packed = jnp.where(keep, total, both)
                 table[a * SPAN + b] = encode(jnp.concatenate([packed, tail], axis=0))
 
-        def mirror_block(a, b):
-            return mirror[a * BLK : (a + 1) * BLK, b * BLK : (b + 1) * BLK].astype(jnp.float32)
-
-        def own_block(a, b):
-            start = pl.multiple_of(own_start + b * BLK, BLK)
-            return matrix[a * BLK : (a + 1) * BLK, pl.ds(start, BLK)].astype(jnp.float32)
+        def block_of(ref, a, b):
+            return ref[a * BLK : (a + 1) * BLK, b * BLK : (b + 1) * BLK].astype(jnp.float32)
 
         for a in range(SPAN):
             for b in range(SPAN):
 
                 @pl.when(flip)
                 def _():
-                    put(a, b, mirror_block(a, b), own_block(b, a))
+                    put(a, b, block_of(mirror, a, b), block_of(own, b, a))
 
                 @pl.when(jnp.logical_not(flip))
                 def _():
-                    put(a, b, own_block(a, b), mirror_block(b, a))
+                    put(a, b, block_of(own, a, b), block_of(mirror, b, a))
 
     def copy(k, carry):
         out[k] = table[index[step * per_step + k]]
@@ -113,8 +106,9 @@
     lax.fori_loop(0, per_step, copy, 0, unroll=4)
 
 
-def pick(flags, index, matrix, mirror):
+def pick(flags, index, own, other, mirror):
     per_step = 16
+    whole = pl.BlockSpec((SLOT, SLOT), lambda s: (0, 0))
     return pl.pallas_call(
         pick_kernel,
         grid=(DEVICES // per_step,),
@@ -122,13 +116,14 @@
         in_specs=[
             pl.BlockSpec(memory_space=pltpu.SMEM),
             pl.BlockSpec(memory_space=pltpu.SMEM),
-            pl.BlockSpec((SLOT, 2 * SLOT), lambda s: (0, 0)),
-            pl.BlockSpec((SLOT, SLOT), lambda s: (0, 0)),
+            whole,
+            whole,
+            whole,
         ],
         out_specs=pl.BlockSpec((per_step, ROWS, BLK), lambda s: (s, 0, 0)),
         scratch_shapes=[pltpu.VMEM((BUCKETS, ROWS, BLK), jnp.int16)],
         compiler_params=pltpu.CompilerParams(vmem_limit_bytes=VMEM_SMALL),
-    )(flags, index, matrix, mirror)
+    )(flags, index, own, other, mirror)
 
 
 def pack(value):
@@ -148,37 +143,34 @@
     count,
     blocks_in,
     basis_in,
-    coarse_in,
+    coarse,
     turned_in,
+    core_in,
+    weights_in,
+    density,
+    pieces,
+    blocks,
+    basis,
+    turned,
     core,
     weights,
-    density,
-    pieces_out,
-    blocks,
-    basis,
-    coarse,
-    turned,
-    pieces,
     high,
     fine,
     total,
     scaled,
     arrived,
-    left_here,
 ):
     def chunk(k, source, target, at):
         lanes = (slice(None), slice(k * CHUNK, (k + 1) * CHUNK))
         return pltpu.make_async_copy(source.at[lanes], target.at[lanes], arrived.at[at])
 
-    chunks = []
-    for k in range(COLS // CHUNK):
-        chunks.append(chunk(k, basis_in, basis, 2 * k))
-        chunks.append(chunk(k, coarse_in, coarse, 2 * k + 1))
+    chunks = [chunk(k, basis_in, basis, k) for k in range(COLS // CHUNK)]
     load_blocks = pltpu.make_async_copy(blocks_in, blocks, arrived.at[len(chunks)])
     load_turned = pltpu.make_async_copy(turned_in, turned, arrived.at[len(chunks) + 1])
+    load_core = pltpu.make_async_copy(core_in, core, arrived.at[len(chunks) + 2])
+    load_weights = pltpu.make_async_copy(weights_in, weights, arrived.at[len(chunks) + 3])
     load_blocks.start()
     chunks[0].start()
-    chunks[1].start()
 
     rows, cols = row_col((BLK, BLK))
 
@@ -217,13 +209,13 @@
     for big in range(KB // 2):
         depth = (big + 1) * PAIR
         if big * PAIR % CHUNK == 0:
-            k = 2 * (big * PAIR // CHUNK)
+            k = big * PAIR // CHUNK
             chunks[k].wait()
-            chunks[k + 1].wait()
-            if k + 2 < len(chunks):
-                chunks[k + 2].start()
-                chunks[k + 3].start()
+            if k + 1 < len(chunks):
+                chunks[k + 1].start()
             else:
+                load_core.start()
+                load_weights.start()
                 load_turned.start()
 
         for m in range(tiles):
@@ -241,6 +233,8 @@
             place_diagonal(big + 1)
 
     summed = jnp.sum(total[...], axis=1, keepdims=True) * (1.0 / STEP)
+    load_core.wait()
+    load_weights.wait()
     found = core[...] + summed
     density[...] = found
     potential = slater_factor * jnp.exp(jnp.log(jnp.maximum(found, density_floor)) * (1.0 / 3.0))
@@ -251,7 +245,6 @@
 
     def send(device, value, last=tail):
         pieces[device] = pack(jnp.concatenate([value, last], axis=0))
-        pltpu.make_async_copy(pieces.at[device], pieces_out.at[device], left_here).start()
 
     def weigh(big, low, high_end):
         for k in range(2):
@@ -284,7 +277,6 @@
                 last = jnp.broadcast_to(diagonal, (ROWS - BLK, BLK))
                 send(i * INNERS + big, jnp.where(rows > cols, cross, product[:BLK, :BLK]), last)
                 send((i + 1) * INNERS + big, jnp.where(rows < cols, cross, product[BLK:, BLK:]), last)
-    pltpu.make_async_copy(pieces, pieces_out, left_here).wait()
 
 
 def batch(count, blocks, basis, coarse, turned, core, weights):
@@ -297,22 +289,21 @@
             jax.ShapeDtypeStruct((PTS, 1), jnp.float32),
             jax.ShapeDtypeStruct(messages, jnp.int16),
         ),
-        in_specs=[pl.BlockSpec(memory_space=pltpu.SMEM)] + [anywhere] * 4 + [vmem] * 2,
-        out_specs=(vmem, pl.BlockSpec(memory_space=pltpu.HBM)),
+        in_specs=[pl.BlockSpec(memory_space=pltpu.SMEM)] + [anywhere, anywhere, vmem, anywhere, anywhere, anywhere],
+        out_specs=(vmem, vmem),
         scratch_shapes=[
             pltpu.VMEM(messages, jnp.int16),
             pltpu.VMEM((PTS, COLS), jnp.bfloat16),
-            pltpu.VMEM((PTS, COLS), jnp.float8_e4m3fn),
             pltpu.VMEM((COLS, PTS), jnp.bfloat16),
-            pltpu.VMEM(messages, jnp.int16),
+            pltpu.VMEM((PTS, 1), jnp.float32),
+            pltpu.VMEM((PTS, 1), jnp.float32),
             pltpu.VMEM((2, COLS, PAIR), jnp.bfloat16),
             pltpu.VMEM((2, COLS, PAIR), jnp.float8_e4m3fn),
             pltpu.VMEM((PTS, BLK), jnp.float32),
             pltpu.VMEM((2, PTS, PAIR), jnp.bfloat16),
-            pltpu.SemaphoreType.DMA((2 * (COLS // CHUNK) + 2,)),
-            pltpu.SemaphoreType.DMA,
+            pltpu.SemaphoreType.DMA((COLS // CHUNK + 4,)),
         ],
-        compiler_params=pltpu.CompilerParams(vmem_limit_bytes=VMEM_ALL),
+        compiler_params=pltpu.CompilerParams(vmem_limit_bytes=VMEM_BATCH),
     )(count, blocks, basis, coarse, turned, core, weights)
 
 
@@ -441,7 +432,9 @@
 
     basis = basis_values[0]
     left, right = density_matrix[:, :SLOT], density_matrix[:, SLOT:]
-    sent = jnp.where((half == 0) == special, left, right)
+    own = jnp.where(half == 0, left, right)
+    other = jnp.where(half == 0, right, left)
+    sent = jnp.where(special, own, other)
     mirror = lax.ppermute(sent, AXES, pairs)
     lists = lax.all_to_all(
         jnp.broadcast_to(block_list, (DEVICES, KB)), AXES, split_axis=0, concat_axis=0, tiled=True
@@ -450,7 +443,7 @@
     factor = jnp.where(slots == first, SPAN, 0) + jnp.where(slots == second, 1, 0)
     index = jnp.sum((lists - slots * SPAN) * factor, axis=1).astype(jnp.int32)
 
-    picked = pick(flags, index, density_matrix, mirror)
+    picked = pick(flags, index, own, other, mirror)
     blocks = lax.all_to_all(picked, AXES, split_axis=0, concat_axis=0, tiled=True)
     density, pieces = batch(
         point_counts,

time: 229 us -> 228 us (level)
  waiting for transfers between devices: 77.1 us -> 74.2 us
  local copies, waits for them, and re-layouts: 21.9 us -> 24.7 us
    unnamed x11 -> x13, local copies, waits for them, and re-layouts: 12 us -> 13 us
  transfers between devices with their start and end apart: 4 -> 4, of which waited for: 3 -> 3; matrix products, arithmetic and copies ran while one was open for 10% -> 12% of each run, Pallas kernels for 0% -> 0%
where the time goes in v2:
time: 228 us; the launch traced here: 227 us
  waiting for transfers between devices  74.2 us (33%)
  blocking collectives  60 us (26%)
  Pallas kernels  36.8 us (16%)
  local copies, waits for them, and re-layouts  24.7 us (11%)
  starting transfers between devices  21.9 us (10%)
  other arithmetic  7.83 us (3%)
    all_to_all x1, blocking collectives, per_device(): lax.all_to_all(pieces, AXES, split_axis=0, concat_axis=0, tiled=True)  60 us
    all_to_all x1, waiting for transfers between devices, per_device(): lax.all_to_all(picked, AXES, split_axis=0, concat_axis=0, tiled=True)  29.3 us
    pallas_call x1, Pallas kernels, batch(): pl.pallas_call(batch_kernel, out_shape=(jax.ShapeDtypeStruct((PTS, 1), jn...  27.4 us
    ppermute x1, waiting for transfers between devices, per_device(): lax.ppermute(copy, AXES, [(target, source) for source, target in pairs])  25.7 us
    all_to_all x1, waiting for transfers between devices, per_device(): lax.all_to_all(jnp.broadcast_to(block_list, (DEVICES, KB)), AXES, split_a...  19.2 us
    unnamed x13, local copies, waits for them, and re-layouts  13 us
    all_to_all x1, starting transfers between devices, per_device(): lax.all_to_all(jnp.broadcast_to(block_list, (DEVICES, KB)), AXES, split_a...  9.46 us
    all_to_all x1, starting transfers between devices, per_device(): lax.all_to_all(picked, AXES, split_axis=0, concat_axis=0, tiled=True)  7.56 us
  transfers between devices with their start and end apart: 4, of which 3 were waited for; matrix products, arithmetic and copies ran while one was open for 12% of the time, Pallas kernels for 0%

profile of v2, /device:TPU:96, one launch (start us, length us, event | category | flops | bytes accessed | tf_op | source)
XLA Modules:
  0.0 226.8 jit_solution(15356556650597673384)
XLA Ops:
  0.7 1.3 broadcast_select_fusion
  2.0 1.7 collective-permute-start
  3.7 1.3 broadcast_in_dim.17
  5.0 9.5 %all-to-all-start = ((s32[128,1,16]{2,1,0:T(1,128)}), s32[128,1,16]{2,1,0:T(1,128)S(1)}, u32[]{:S(2)}, u32[]{:S(2)}) async-start(s32[128,1,16]{2,1,0:T(1,128)} %broadcast_in_dim.17), calls=%async_computation | async-start | bytes 131072 | tf_op jit(solution)/shard_map/all_to_all | solution.py:439
  14.5 0.1 pad_add_fusion.flags
  14.6 19.2 %all-to-all-done = s32[128,1,16]{2,1,0:T(1,128)S(1)} async-done(((s32[128,1,16]{2,1,0:T(1,128)}), s32[128,1,16]{2,1,0:T(1,128)S(1)}, u32[]{:S(2)}, u32[]{:S(2)}) %all-to-all-start) | async-done | bytes 8224 | tf_op jit(solution)/shard_map/all_to_all | solution.py:439
  33.9 0.1 fusion.1.index
  33.9 0.0 collective-permute-done.mirror
  34.0 3.1 %shard_map.80 = s16[128,136,128]{2,1,0:T(8,128)(2,1)S(1)} custom-call(s32[4]{0:T(128)S(1)} %pad_add_fusion.flags, s32[128]{0:T(128)S(1)} %fusion.1.index, bf16[512,512]{1,0:T(8,128)(2,1)S(1)} %get-tuple-element.12.own, bf16[512,512]{1,0:T(8,128)(2,1)S(1)} %get-tuple-element.11.other, bf16[512,512]{1,0:T(8,128)(2,1)S(1)} %collective-permute-done.mirror), custom_call_target="tpu_custom_call" | custom-call | tf_op jit(solution)/shard_map/pallas_call | solution.py:112
  37.1 0.0 copy-start
  37.1 2.1 copy-done
  39.2 0.0 copy-start.4
  39.2 0.0 copy-start.5
  39.2 7.6 %all-to-all-start.1 = ((s16[128,136,128]{2,1,0:T(8,128)(2,1)}), s16[128,136,128]{2,1,0:T(8,128)(2,1)}, u32[]{:S(2)}, u32[]{:S(2)}) async-start(s16[128,136,128]{2,1,0:T(8,128)(2,1)} %copy-done), calls=%async_computation.1 | async-start | bytes 8912896 | tf_op jit(solution)/shard_map/all_to_all | solution.py:447
  47.4 0.0 copy-done.4
  47.5 1.2 copy.31.core_in
  48.6 0.0 copy-done.5
  48.6 1.2 copy.32.weights_in
  49.9 8.6 %copy.28 = bf16[1,1536,2048]{1,2,0:T(8,128)(2,1)} copy(bf16[1,1536,2048]{2,1,0:T(8,128)(2,1)} %param.7) | data formatting | bytes 12582912 | tf_op args[1]
  58.5 4.9 %bitcast_convert_fusion = f8e4m3fn[1536,2048]{0,1:T(32,128)(4,1)S(1)} fusion(bf16[1,1536,2048]{1,2,0:T(8,128)(2,1)} %copy.28), kind=kLoop, calls=%fused_computation | loop fusion | flops 3145728 | bytes 9437184 | tf_op jit(solution)/shard_map/convert_element_type | solution.py:452
  63.4 7.2 %copy.30.coarse = f8e4m3fn[1536,2048]{1,0:T(32,128)(4,1)S(1)} copy(f8e4m3fn[1536,2048]{0,1:T(32,128)(4,1)S(1)} %bitcast_convert_fusion) | data formatting | bytes 6291456 | tf_op jit(solution)/shard_map/convert_element_type | solution.py:452
  70.7 29.3 %all-to-all-done.1.blocks_in = s16[128,136,128]{2,1,0:T(8,128)(2,1)} async-done(((s16[128,136,128]{2,1,0:T(8,128)(2,1)}), s16[128,136,128]{2,1,0:T(8,128)(2,1)}, u32[]{:S(2)}, u32[]{:S(2)}) %all-to-all-start.1) | async-done | bytes 4456480 | tf_op jit(solution)/shard_map/all_to_all | solution.py:447
  100.0 0.0 copy-start.1
  100.0 1.1 copy-done.1
  101.1 0.0 copy-start.2
  101.1 1.1 copy-done.2
  102.2 27.4 %shard_map.81 = (f32[1536,1]{1,0:T(8,128)S(1)}, s16[128,136,128]{2,1,0:T(8,128)(2,1)S(1)}) custom-call(s32[1]{0:T(128)S(6)} %copy.34.count, s16[128,136,128]{2,1,0:T(8,128)(2,1)} %all-to-all-done.1.blocks_in, bf16[1536,2048]{1,0:T(8,128)(2,1)} %bitcast.19, f8e4m3fn[1536,2048]{1,0:T(32,128)(4,1)S(1)} %copy.30.coarse, bf16[2048,1536]{1,0:T(8,128)(2,1)} %bitcast.18, ...), custom_call_target="tpu_custom_call" | custom-call | tf_op jit(solution)/shard_map/pallas_call | solution.py:286
  129.7 0.0 copy-start.3
  129.7 60.0 %all_to_all.19.pieces = s16[128,136,128]{2,1,0:T(8,128)(2,1)S(1)} all-to-all(s16[128,136,128]{2,1,0:T(8,128)(2,1)S(1)} %get-tuple-element.7), channel_id=1, replica_groups=mesh['group'=16,'inner'=8] {'group','inner'}, dimensions={0} | all-to-all | bytes 8912896 | tf_op jit(solution)/shard_map/all_to_all | solution.py:457
  189.7 0.0 copy-done.3
  189.7 2.6 %shard_map.82 = (f32[16,136,128]{2,1,0:T(8,128)S(1)}, s16[16,136,128]{2,1,0:T(8,128)(2,1)S(1)}) custom-call(s32[128]{0:T(128)S(1)} %fusion.1.index, s16[128,136,128]{2,1,0:T(8,128)(2,1)S(1)} %all_to_all.19.pieces), custom_call_target="tpu_custom_call" | custom-call | tf_op jit(solution)/shard_map/pallas_call | solution.py:335
  192.3 3.1 %collective-permute-start.1 = (s16[16,136,128]{2,1,0:T(8,128)(2,1)S(1)}, s16[16,136,128]{2,1,0:T(8,128)(2,1)S(1)}, u32[]{:S(2)}, u32[]{:S(2)}) collective-permute-start(s16[16,136,128]{2,1,0:T(8,128)(2,1)S(1)} %get-tuple-element.9), channel_id=1, source_target_pairs={{8,0},{24,1},{40,2},{56,3},{72,4},{88,5},{104,6},{120,7},{0,8},{16... | collective-permute-start | bytes 1671176 | tf_op jit(solution)/shard_map/ppermute | solution.py:459
  195.5 1.4 reduce
  196.9 0.6 reshape.34
  197.5 25.7 %collective-permute-done.1.mirror = s16[16,136,128]{2,1,0:T(8,128)(2,1)S(1)} collective-permute-done((s16[16,136,128]{2,1,0:T(8,128)(2,1)S(1)}, s16[16,136,128]{2,1,0:T(8,128)(2,1)S(1)}, u32[]{:S(2)}, u32[]{:S(2)}) %collective-permute-start.1) | collective-permute-done | bytes 557088 | tf_op jit(solution)/shard_map/ppermute | solution.py:459
  223.2 3.7 %shard_map.83 = f32[512,1024]{1,0:T(8,128)} custom-call(s32[4]{0:T(128)S(1)} %pad_add_fusion.flags, f32[16,136,128]{2,1,0:T(8,128)S(1)} %get-tuple-element.8.total, s16[16,136,128]{2,1,0:T(8,128)(2,1)S(1)} %collective-permute-done.1.mirror), custom_call_target="tpu_custom_call" | custom-call | tf_op jit(solution)/shard_map/pallas_call | solution.py:412
  (2 shorter events, 0.1 us)
Async XLA Ops:
  2.0 32.0 %collective-permute-start = (bf16[512,512]{1,0:T(8,128)(2,1)S(1)}, bf16[512,512]{1,0:T(8,128)(2,1)S(1)}, u32[]{:S(2)}, u32[]{:S(2)}) collective-permute-start(bf16[512,512]{1,0:T(8,128)(2,1)S(1)} %get-tuple-element.10), channel_id=1, source_target_pairs={{0,8},{1,24},{2,40},{3,56},{4,72},{5,88},{6,104},{7,120},{8,0},{9,... | collective-permute-start | bytes 1572872 | tf_op jit(solution)/shard_map/ppermute | solution.py:438
  5.0 28.8 %all-to-all-start = ((s32[128,1,16]{2,1,0:T(1,128)}), s32[128,1,16]{2,1,0:T(1,128)S(1)}, u32[]{:S(2)}, u32[]{:S(2)}) async-start(s32[128,1,16]{2,1,0:T(1,128)} %broadcast_in_dim.17), calls=%async_computation | async-start | bytes 131072 | tf_op jit(solution)/shard_map/all_to_all | solution.py:439
  37.1 2.1 copy-start
  39.2 8.2 %copy-start.4 = (f32[1,1536]{1,0:T(1,128)S(1)}, f32[1,1536]{1,0:T(1,128)}, u32[]{:S(2)}) copy-start(f32[1,1536]{1,0:T(1,128)} %param.10) | copy-start | bytes 18436
  39.2 9.4 %copy-start.5 = (f32[1,1536]{1,0:T(1,128)S(1)}, f32[1,1536]{1,0:T(1,128)}, u32[]{:S(2)}) copy-start(f32[1,1536]{1,0:T(1,128)} %param.11) | copy-start | bytes 18436
  39.2 60.8 %all-to-all-start.1 = ((s16[128,136,128]{2,1,0:T(8,128)(2,1)}), s16[128,136,128]{2,1,0:T(8,128)(2,1)}, u32[]{:S(2)}, u32[]{:S(2)}) async-start(s16[128,136,128]{2,1,0:T(8,128)(2,1)} %copy-done), calls=%async_computation.1 | async-start | bytes 8912896 | tf_op jit(solution)/shard_map/all_to_all | solution.py:447
  100.0 1.1 copy-start.1
  101.1 1.1 copy-start.2
  129.7 60.0 %copy-start.3 = (f32[1536,1]{1,0:T(8,128)}, f32[1536,1]{1,0:T(8,128)S(1)}, u32[]{:S(2)}) copy-start(f32[1536,1]{1,0:T(8,128)S(1)} %get-tuple-element.6) | copy-start | bytes 18436
  192.3 30.8 %collective-permute-start.1 = (s16[16,136,128]{2,1,0:T(8,128)(2,1)S(1)}, s16[16,136,128]{2,1,0:T(8,128)(2,1)S(1)}, u32[]{:S(2)}, u32[]{:S(2)}) collective-permute-start(s16[16,136,128]{2,1,0:T(8,128)(2,1)S(1)} %get-tuple-element.9), channel_id=1, source_target_pairs={{8,0},{24,1},{40,2},{56,3},{72,4},{88,5},{104,6},{120,7},{0,8},{16... | collective-permute-start | bytes 1671176 | tf_op jit(solution)/shard_map/ppermute | solution.py:459

commit v3 on v2

--- a/solution.py
+++ b/solution.py
@@ -15,6 +15,7 @@
 BUCKETS = SPAN * SPAN
 ROWS = BLK + 8
 PTS = 1536
+LINES = PTS // BLK
 COLS = KB * BLK
 PAIR = 2 * BLK
 AXES = ("group", "inner")
@@ -59,68 +60,56 @@
 
 
 def pick_kernel(flags, index, own, other, mirror, out, table):
-    step = pl.program_id(0)
-    per_step = out.shape[0]
-
-    @pl.when(step == 0)
-    def _():
-        flip = flags[0] == 1
-        special = flags[1] == 1
-        low = flags[2] == 1
-
-        def put(a, b, first, second):
-            rows, cols = row_col((BLK, BLK))
-            total = first + second.T
-            diagonal = jnp.sum(jnp.where(rows == cols, total, 0.0), axis=0, keepdims=True)
-            tail = jnp.broadcast_to(diagonal, (ROWS - BLK, BLK))
-            table[a * SPAN + b] = encode(jnp.concatenate([total, tail], axis=0))
-
-            @pl.when(special)
+    flip = flags[0] == 1
+    special = flags[1] == 1
+    low = flags[2] == 1
+
+    def put(a, b, first, second):
+        rows, cols = row_col((BLK, BLK))
+        total = first + second.T
+        diagonal = jnp.sum(jnp.where(rows == cols, total, 0.0), axis=0, keepdims=True)
+        tail = jnp.broadcast_to(diagonal, (ROWS - BLK, BLK))
+        table[a * SPAN + b] = encode(jnp.concatenate([total, tail], axis=0))
+
+        @pl.when(special)
+        def _():
+            at = jnp.where(low, a, b)
+            start = pl.multiple_of(at * BLK, BLK)
+            block = other[pl.ds(start, BLK), pl.ds(start, BLK)].astype(jnp.float32)
+            both = jnp.where(rows == cols, block, block + block.T)
+            keep = jnp.where(low, rows - cols, cols - rows) > 0
+            packed = jnp.where(keep, total, both)
+            table[a * SPAN + b] = encode(jnp.concatenate([packed, tail], axis=0))
+
+    def block_of(ref, a, b):
+        return ref[a * BLK : (a + 1) * BLK, b * BLK : (b + 1) * BLK].astype(jnp.float32)
+
+    for a in range(SPAN):
+        for b in range(SPAN):
+
+            @pl.when(flip)
             def _():
-                at = jnp.where(low, a, b)
-                start = pl.multiple_of(at * BLK, BLK)
-                block = other[pl.ds(start, BLK), pl.ds(start, BLK)].astype(jnp.float32)
-                both = jnp.where(rows == cols, block, block + block.T)
-                keep = jnp.where(low, rows - cols, cols - rows) > 0
-                packed = jnp.where(keep, total, both)
-                table[a * SPAN + b] = encode(jnp.concatenate([packed, tail], axis=0))
-
-        def block_of(ref, a, b):
-            return ref[a * BLK : (a + 1) * BLK, b * BLK : (b + 1) * BLK].astype(jnp.float32)
-
-        for a in range(SPAN):
-            for b in range(SPAN):
-
-                @pl.when(flip)
-                def _():
-                    put(a, b, block_of(mirror, a, b), block_of(own, b, a))
-
-                @pl.when(jnp.logical_not(flip))
-                def _():
-                    put(a, b, block_of(own, a, b), block_of(mirror, b, a))
+                put(a, b, block_of(mirror, a, b), block_of(own, b, a))
+
+            @pl.when(jnp.logical_not(flip))
+            def _():
+                put(a, b, block_of(own, a, b), block_of(mirror, b, a))
 
     def copy(k, carry):
-        out[k] = table[index[step * per_step + k]]
+        out[k] = table[index[k]]
         return carry
 
-    lax.fori_loop(0, per_step, copy, 0, unroll=4)
+    lax.fori_loop(0, DEVICES, copy, 0, unroll=4)
 
 
 def pick(flags, index, own, other, mirror):
-    per_step = 16
-    whole = pl.BlockSpec((SLOT, SLOT), lambda s: (0, 0))
+    vmem = pl.BlockSpec(memory_space=pltpu.VMEM)
+    smem = pl.BlockSpec(memory_space=pltpu.SMEM)
     return pl.pallas_call(
         pick_kernel,
-        grid=(DEVICES // per_step,),
         out_shape=jax.ShapeDtypeStruct((DEVICES, ROWS, BLK), jnp.int16),
-        in_specs=[
-            pl.BlockSpec(memory_space=pltpu.SMEM),
-            pl.BlockSpec(memory_space=pltpu.SMEM),
-            whole,
-            whole,
-            whole,
-        ],
-        out_specs=pl.BlockSpec((per_step, ROWS, BLK), lambda s: (s, 0, 0)),
+        in_specs=[smem, smem, vmem, vmem, vmem],
+        out_specs=vmem,
         scratch_shapes=[pltpu.VMEM((BUCKETS, ROWS, BLK), jnp.int16)],
         compiler_params=pltpu.CompilerParams(vmem_limit_bytes=VMEM_SMALL),
     )(flags, index, own, other, mirror)
@@ -145,15 +134,13 @@
     basis_in,
     coarse,
     turned_in,
-    core_in,
-    weights_in,
+    core,
+    weights,
     density,
     pieces,
     blocks,
     basis,
     turned,
-    core,
-    weights,
     high,
     fine,
     total,
@@ -167,8 +154,6 @@
     chunks = [chunk(k, basis_in, basis, k) for k in range(COLS // CHUNK)]
     load_blocks = pltpu.make_async_copy(blocks_in, blocks, arrived.at[len(chunks)])
     load_turned = pltpu.make_async_copy(turned_in, turned, arrived.at[len(chunks) + 1])
-    load_core = pltpu.make_async_copy(core_in, core, arrived.at[len(chunks) + 2])
-    load_weights = pltpu.make_async_copy(weights_in, weights, arrived.at[len(chunks) + 3])
     load_blocks.start()
     chunks[0].start()
 
@@ -214,8 +199,6 @@
             if k + 1 < len(chunks):
                 chunks[k + 1].start()
             else:
-                load_core.start()
-                load_weights.start()
                 load_turned.start()
 
         for m in range(tiles):
@@ -232,14 +215,15 @@
         if big + 1 < KB // 2:
             place_diagonal(big + 1)
 
-    summed = jnp.sum(total[...], axis=1, keepdims=True) * (1.0 / STEP)
-    load_core.wait()
-    load_weights.wait()
-    found = core[...] + summed
+    lines = [slice(k * BLK, (k + 1) * BLK) for k in range(LINES)]
+    summed = jnp.concatenate([jnp.sum(total[at].T, axis=0, keepdims=True) for at in lines], axis=0)
+    found = core[...] + summed * (1.0 / STEP)
     density[...] = found
     potential = slater_factor * jnp.exp(jnp.log(jnp.maximum(found, density_floor)) * (1.0 / 3.0))
-    live = lax.broadcasted_iota(jnp.int32, (PTS, 1), 0) < count[0]
-    total[...] = jnp.broadcast_to(jnp.where(live, weights[...] * potential, 0.0), (PTS, BLK))
+    line, lane = row_col((LINES, BLK))
+    integrand = jnp.where(line * BLK + lane < count[0], weights[...] * potential, 0.0)
+    for k, at in enumerate(lines):
+        total[at] = jnp.broadcast_to(integrand[k : k + 1], (BLK, BLK)).T
 
     tail = jnp.zeros((ROWS - BLK, BLK), jnp.float32)
 
@@ -286,61 +270,46 @@
     return pl.pallas_call(
         batch_kernel,
         out_shape=(
-            jax.ShapeDtypeStruct((PTS, 1), jnp.float32),
+            jax.ShapeDtypeStruct((LINES, BLK), jnp.float32),
             jax.ShapeDtypeStruct(messages, jnp.int16),
         ),
-        in_specs=[pl.BlockSpec(memory_space=pltpu.SMEM)] + [anywhere, anywhere, vmem, anywhere, anywhere, anywhere],
+        in_specs=[pl.BlockSpec(memory_space=pltpu.SMEM)] + [anywhere, anywhere, vmem, anywhere, vmem, vmem],
         out_specs=(vmem, vmem),
         scratch_shapes=[
             pltpu.VMEM(messages, jnp.int16),
             pltpu.VMEM((PTS, COLS), jnp.bfloat16),
             pltpu.VMEM((COLS, PTS), jnp.bfloat16),
-            pltpu.VMEM((PTS, 1), jnp.float32),
-            pltpu.VMEM((PTS, 1), jnp.float32),
             pltpu.VMEM((2, COLS, PAIR), jnp.bfloat16),
             pltpu.VMEM((2, COLS, PAIR), jnp.float8_e4m3fn),
             pltpu.VMEM((PTS, BLK), jnp.float32),
             pltpu.VMEM((2, PTS, PAIR), jnp.bfloat16),
-            pltpu.SemaphoreType.DMA((COLS // CHUNK + 4,)),
+            pltpu.SemaphoreType.DMA((COLS // CHUNK + 2,)),
         ],
         compiler_params=pltpu.CompilerParams(vmem_limit_bytes=VMEM_BATCH),
     )(count, blocks, basis, coarse, turned, core, weights)
 
 
 def sum_kernel(index, pieces, total, copy):
-    step = pl.program_id(0)
-    per_step = pieces.shape[0]
-
-    @pl.when(step == 0)
-    def _():
-        total[...] = jnp.zeros_like(total)
+    total[...] = jnp.zeros_like(total)
 
     def add(k, carry):
-        at = index[step * per_step + k]
+        at = index[k]
         total[at] = total[at] + unpack(pieces[k])
         return carry
 
-    lax.fori_loop(0, per_step, add, 0, unroll=4)
-
-    @pl.when(step == pl.num_programs(0) - 1)
-    def _():
-        for k in range(BUCKETS):
-            copy[k] = pack(total[k])
+    lax.fori_loop(0, DEVICES, add, 0, unroll=4)
+    for k in range(BUCKETS):
+        copy[k] = pack(total[k])
 
 
 def sum_pieces(index, pieces):
-    per_step = 16
     shape = (BUCKETS, ROWS, BLK)
-    whole = pl.BlockSpec(shape, lambda s: (0, 0, 0))
+    vmem = pl.BlockSpec(memory_space=pltpu.VMEM)
     return pl.pallas_call(
         sum_kernel,
-        grid=(DEVICES // per_step,),
         out_shape=(jax.ShapeDtypeStruct(shape, jnp.float32), jax.ShapeDtypeStruct(shape, jnp.int16)),
-        in_specs=[
-            pl.BlockSpec(memory_space=pltpu.SMEM),
-            pl.BlockSpec((per_step, ROWS, BLK), lambda s: (s, 0, 0)),
-        ],
-        out_specs=(whole, whole),
+        in_specs=[pl.BlockSpec(memory_space=pltpu.SMEM), vmem],
+        out_specs=(vmem, vmem),
         compiler_params=pltpu.CompilerParams(vmem_limit_bytes=VMEM_SMALL),
     )(index, pieces)
 
@@ -451,8 +420,8 @@
         basis,
         basis.astype(jnp.float8_e4m3fn),
         basis.T,
-        core_density.reshape(PTS, 1),
-        grid_weights.reshape(PTS, 1),
+        core_density.reshape(LINES, BLK),
+        grid_weights.reshape(LINES, BLK),
     )
     landed = lax.all_to_all(pieces, AXES, split_axis=0, concat_axis=0, tiled=True)
     total, copy = sum_pieces(index, landed)

time: 228 us -> 225 us (0.987)
  local copies, waits for them, and re-layouts: 24.7 us -> 20.1 us
  waiting for transfers between devices: 74.2 us -> 77.8 us
    reshape x3 -> x0, local copies, waits for them, and re-layouts: 3 us -> none  [the longest x1 1.21 us: per_device(): grid_weights.reshape(PTS, 1)]
    unnamed x13 -> x8, local copies, waits for them, and re-layouts: 13 us -> 11.4 us
  transfers between devices with their start and end apart: 4 -> 4, of which waited for: 3 -> 3; matrix products, arithmetic and copies ran while one was open for 12% -> 10% of each run, Pallas kernels for 0% -> 0%
where the time goes in v3:
time: 225 us; the launch traced here: 224 us
  waiting for transfers between devices  77.8 us (35%)
  blocking collectives  60 us (27%)
  Pallas kernels  36.8 us (16%)
  starting transfers between devices  21.8 us (10%)
  local copies, waits for them, and re-layouts  20.1 us (9%)
  other arithmetic  6.47 us (3%)
    all_to_all x1, blocking collectives, per_device(): lax.all_to_all(pieces, AXES, split_axis=0, concat_axis=0, tiled=True)  60 us
    all_to_all x1, waiting for transfers between devices, per_device(): lax.all_to_all(picked, AXES, split_axis=0, concat_axis=0, tiled=True)  31.5 us
    pallas_call x1, Pallas kernels, batch(): pl.pallas_call(batch_kernel, out_shape=(jax.ShapeDtypeStruct((LINES, BLK)...  27.8 us
    ppermute x1, waiting for transfers between devices, per_device(): lax.ppermute(copy, AXES, [(target, source) for source, target in pairs])  27.1 us
    all_to_all x1, waiting for transfers between devices, per_device(): lax.all_to_all(jnp.broadcast_to(block_list, (DEVICES, KB)), AXES, split_a...  19.2 us
    unnamed x8, local copies, waits for them, and re-layouts  11.4 us
    all_to_all x1, starting transfers between devices, per_device(): lax.all_to_all(jnp.broadcast_to(block_list, (DEVICES, KB)), AXES, split_a...  9.46 us
    all_to_all x1, starting transfers between devices, per_device(): lax.all_to_all(picked, AXES, split_axis=0, concat_axis=0, tiled=True)  7.55 us
  transfers between devices with their start and end apart: 4, of which 3 were waited for; matrix products, arithmetic and copies ran while one was open for 10% of the time, Pallas kernels for 0%

profile of v3, /device:TPU:96, one launch (start us, length us, event | category | flops | bytes accessed | tf_op | source)
XLA Modules:
  0.0 224.5 jit_solution(1066393069078826018)
XLA Ops:
  0.7 1.3 broadcast_select_fusion
  2.0 1.7 collective-permute-start
  3.7 1.3 broadcast_in_dim.17
  5.0 9.5 %all-to-all-start = ((s32[128,1,16]{2,1,0:T(1,128)}), s32[128,1,16]{2,1,0:T(1,128)S(1)}, u32[]{:S(2)}, u32[]{:S(2)}) async-start(s32[128,1,16]{2,1,0:T(1,128)} %broadcast_in_dim.17), calls=%async_computation | async-start | bytes 131072 | tf_op jit(solution)/shard_map/all_to_all | solution.py:408
  14.5 0.1 pad_add_fusion.flags
  14.6 19.2 %all-to-all-done = s32[128,1,16]{2,1,0:T(1,128)S(1)} async-done(((s32[128,1,16]{2,1,0:T(1,128)}), s32[128,1,16]{2,1,0:T(1,128)S(1)}, u32[]{:S(2)}, u32[]{:S(2)}) %all-to-all-start) | async-done | bytes 8224 | tf_op jit(solution)/shard_map/all_to_all | solution.py:408
  33.9 0.1 fusion.1.index
  33.9 0.0 collective-permute-done.mirror
  34.0 2.9 %shard_map.80 = s16[128,136,128]{2,1,0:T(8,128)(2,1)S(1)} custom-call(s32[4]{0:T(128)S(1)} %pad_add_fusion.flags, s32[128]{0:T(128)S(1)} %fusion.1.index, bf16[512,512]{1,0:T(8,128)(2,1)S(1)} %get-tuple-element.12.own, bf16[512,512]{1,0:T(8,128)(2,1)S(1)} %get-tuple-element.11.other, bf16[512,512]{1,0:T(8,128)(2,1)S(1)} %collective-permute-done.mirror), custom_call_target="tpu_custom_call" | custom-call | tf_op jit(solution)/shard_map/pallas_call | solution.py:108
  36.9 0.0 copy-start
  36.9 2.1 copy-done
  39.0 0.0 copy-start.1
  39.0 0.0 copy-start.2
  39.0 7.6 %all-to-all-start.1 = ((s16[128,136,128]{2,1,0:T(8,128)(2,1)}), s16[128,136,128]{2,1,0:T(8,128)(2,1)}, u32[]{:S(2)}, u32[]{:S(2)}) async-start(s16[128,136,128]{2,1,0:T(8,128)(2,1)} %copy-done), calls=%async_computation.1 | async-start | bytes 8912896 | tf_op jit(solution)/shard_map/all_to_all | solution.py:416
  47.2 0.0 copy-done.1
  47.2 0.0 copy-done.2
  47.3 8.6 %copy.19 = bf16[1,1536,2048]{1,2,0:T(8,128)(2,1)} copy(bf16[1,1536,2048]{2,1,0:T(8,128)(2,1)} %param.7) | data formatting | bytes 12582912 | tf_op args[1]
  55.9 4.9 %bitcast_convert_fusion = f8e4m3fn[1536,2048]{0,1:T(32,128)(4,1)S(1)} fusion(bf16[1,1536,2048]{1,2,0:T(8,128)(2,1)} %copy.19), kind=kLoop, calls=%fused_computation | loop fusion | flops 3145728 | bytes 9437184 | tf_op jit(solution)/shard_map/convert_element_type | solution.py:421
  60.9 7.4 %copy.21.coarse = f8e4m3fn[1536,2048]{1,0:T(32,128)(4,1)S(1)} copy(f8e4m3fn[1536,2048]{0,1:T(32,128)(4,1)S(1)} %bitcast_convert_fusion) | data formatting | bytes 6291456 | tf_op jit(solution)/shard_map/convert_element_type | solution.py:421
  68.3 31.5 %all-to-all-done.1.blocks_in = s16[128,136,128]{2,1,0:T(8,128)(2,1)} async-done(((s16[128,136,128]{2,1,0:T(8,128)(2,1)}), s16[128,136,128]{2,1,0:T(8,128)(2,1)}, u32[]{:S(2)}, u32[]{:S(2)}) %all-to-all-start.1) | async-done | bytes 4456480 | tf_op jit(solution)/shard_map/all_to_all | solution.py:416
  99.7 27.8 %shard_map.81 = (f32[12,128]{1,0:T(8,128)S(1)}, s16[128,136,128]{2,1,0:T(8,128)(2,1)S(1)}) custom-call(s32[1]{0:T(128)S(6)} %copy.26.count, s16[128,136,128]{2,1,0:T(8,128)(2,1)} %all-to-all-done.1.blocks_in, bf16[1536,2048]{1,0:T(8,128)(2,1)} %bitcast.27, f8e4m3fn[1536,2048]{1,0:T(32,128)(4,1)S(1)} %copy.21.coarse, bf16[2048,1536]{1,0:T(8,128)(2,1)} %bitcast.26, ...), custom_call_target="tpu_custom_call" | custom-call | tf_op jit(solution)/shard_map/pallas_call | solution.py:270
  127.5 60.0 %all_to_all.19.pieces = s16[128,136,128]{2,1,0:T(8,128)(2,1)S(1)} all-to-all(s16[128,136,128]{2,1,0:T(8,128)(2,1)S(1)} %get-tuple-element.7), channel_id=1, replica_groups=mesh['group'=16,'inner'=8] {'group','inner'}, dimensions={0} | all-to-all | bytes 8912896 | tf_op jit(solution)/shard_map/all_to_all | solution.py:426
  187.5 2.4 %shard_map.82 = (f32[16,136,128]{2,1,0:T(8,128)S(1)}, s16[16,136,128]{2,1,0:T(8,128)(2,1)S(1)}) custom-call(s32[128]{0:T(128)S(1)} %fusion.1.index, s16[128,136,128]{2,1,0:T(8,128)(2,1)S(1)} %all_to_all.19.pieces), custom_call_target="tpu_custom_call" | custom-call | tf_op jit(solution)/shard_map/pallas_call | solution.py:308
  190.0 3.1 %collective-permute-start.1 = (s16[16,136,128]{2,1,0:T(8,128)(2,1)S(1)}, s16[16,136,128]{2,1,0:T(8,128)(2,1)S(1)}, u32[]{:S(2)}, u32[]{:S(2)}) collective-permute-start(s16[16,136,128]{2,1,0:T(8,128)(2,1)S(1)} %get-tuple-element.9), channel_id=1, source_target_pairs={{8,0},{24,1},{40,2},{56,3},{72,4},{88,5},{104,6},{120,7},{0,8},{16... | collective-permute-start | bytes 1671176 | tf_op jit(solution)/shard_map/ppermute | solution.py:428
  193.1 0.6 copy.25
  193.7 27.1 %collective-permute-done.1.mirror = s16[16,136,128]{2,1,0:T(8,128)(2,1)S(1)} collective-permute-done((s16[16,136,128]{2,1,0:T(8,128)(2,1)S(1)}, s16[16,136,128]{2,1,0:T(8,128)(2,1)S(1)}, u32[]{:S(2)}, u32[]{:S(2)}) %collective-permute-start.1) | collective-permute-done | bytes 557088 | tf_op jit(solution)/shard_map/ppermute | solution.py:428
  220.8 3.7 %shard_map.83 = f32[512,1024]{1,0:T(8,128)} custom-call(s32[4]{0:T(128)S(1)} %pad_add_fusion.flags, f32[16,136,128]{2,1,0:T(8,128)S(1)} %get-tuple-element.8.total, s16[16,136,128]{2,1,0:T(8,128)(2,1)S(1)} %collective-permute-done.1.mirror), custom_call_target="tpu_custom_call" | custom-call | tf_op jit(solution)/shard_map/pallas_call | solution.py:381
  (4 shorter events, 0.1 us)
Async XLA Ops:
  2.0 32.0 %collective-permute-start = (bf16[512,512]{1,0:T(8,128)(2,1)S(1)}, bf16[512,512]{1,0:T(8,128)(2,1)S(1)}, u32[]{:S(2)}, u32[]{:S(2)}) collective-permute-start(bf16[512,512]{1,0:T(8,128)(2,1)S(1)} %get-tuple-element.10), channel_id=1, source_target_pairs={{0,8},{1,24},{2,40},{3,56},{4,72},{5,88},{6,104},{7,120},{8,0},{9,... | collective-permute-start | bytes 1572872 | tf_op jit(solution)/shard_map/ppermute | solution.py:407
  5.0 28.8 %all-to-all-start = ((s32[128,1,16]{2,1,0:T(1,128)}), s32[128,1,16]{2,1,0:T(1,128)S(1)}, u32[]{:S(2)}, u32[]{:S(2)}) async-start(s32[128,1,16]{2,1,0:T(1,128)} %broadcast_in_dim.17), calls=%async_computation | async-start | bytes 131072 | tf_op jit(solution)/shard_map/all_to_all | solution.py:408
  36.9 2.1 copy-start
  39.0 8.2 %copy-start.1 = (f32[1,1536]{1,0:T(1,128)S(1)}, f32[1,1536]{1,0:T(1,128)}, u32[]{:S(2)}) copy-start(f32[1,1536]{1,0:T(1,128)} %param.10) | copy-start | bytes 18436
  39.0 8.3 %copy-start.2 = (f32[1,1536]{1,0:T(1,128)S(1)}, f32[1,1536]{1,0:T(1,128)}, u32[]{:S(2)}) copy-start(f32[1,1536]{1,0:T(1,128)} %param.11) | copy-start | bytes 18436
  39.0 60.8 %all-to-all-start.1 = ((s16[128,136,128]{2,1,0:T(8,128)(2,1)}), s16[128,136,128]{2,1,0:T(8,128)(2,1)}, u32[]{:S(2)}, u32[]{:S(2)}) async-start(s16[128,136,128]{2,1,0:T(8,128)(2,1)} %copy-done), calls=%async_computation.1 | async-start | bytes 8912896 | tf_op jit(solution)/shard_map/all_to_all | solution.py:416
  190.0 30.8 %collective-permute-start.1 = (s16[16,136,128]{2,1,0:T(8,128)(2,1)S(1)}, s16[16,136,128]{2,1,0:T(8,128)(2,1)S(1)}, u32[]{:S(2)}, u32[]{:S(2)}) collective-permute-start(s16[16,136,128]{2,1,0:T(8,128)(2,1)S(1)} %get-tuple-element.9), channel_id=1, source_target_pairs={{8,0},{24,1},{40,2},{56,3},{72,4},{88,5},{104,6},{120,7},{0,8},{16... | collective-permute-start | bytes 1671176 | tf_op jit(solution)/shard_map/ppermute | solution.py:428

commit v4 on v3

--- a/solution.py
+++ b/solution.py
@@ -67,12 +67,16 @@
     def put(a, b, first, second):
         rows, cols = row_col((BLK, BLK))
         total = first + second.T
-        diagonal = jnp.sum(jnp.where(rows == cols, total, 0.0), axis=0, keepdims=True)
-        tail = jnp.broadcast_to(diagonal, (ROWS - BLK, BLK))
-        table[a * SPAN + b] = encode(jnp.concatenate([total, tail], axis=0))
+
+        @pl.when(jnp.logical_not(special))
+        def _():
+            tail = jnp.zeros((ROWS - BLK, BLK), jnp.float32)
+            table[a * SPAN + b] = encode(jnp.concatenate([total, tail], axis=0))
 
         @pl.when(special)
         def _():
+            diagonal = jnp.sum(jnp.where(rows == cols, total, 0.0), axis=0, keepdims=True)
+            tail = jnp.broadcast_to(diagonal, (ROWS - BLK, BLK))
             at = jnp.where(low, a, b)
             start = pl.multiple_of(at * BLK, BLK)
             block = other[pl.ds(start, BLK), pl.ds(start, BLK)].astype(jnp.float32)
@@ -99,7 +103,7 @@
         out[k] = table[index[k]]
         return carry
 
-    lax.fori_loop(0, DEVICES, copy, 0, unroll=4)
+    lax.fori_loop(0, DEVICES, copy, 0, unroll=8)
 
 
 def pick(flags, index, own, other, mirror):
@@ -297,7 +301,7 @@
         total[at] = total[at] + unpack(pieces[k])
         return carry
 
-    lax.fori_loop(0, DEVICES, add, 0, unroll=4)
+    lax.fori_loop(0, DEVICES, add, 0, unroll=8)
     for k in range(BUCKETS):
         copy[k] = pack(total[k])
 
@@ -314,7 +318,46 @@
     )(index, pieces)
 
 
-def finish_kernel(flags, total, mirror, out):
+def half_of(ref, which):
+    return ref.at[:, pl.ds(pl.multiple_of(which * SLOT, SLOT), SLOT)]
+
+
+def lay_out(flip, held, block_of):
+    for a in range(SPAN):
+        for b in range(SPAN):
+            k = a * SPAN + b
+
+            @pl.when(flip)
+            def _():
+                held[b * BLK : (b + 1) * BLK, a * BLK : (a + 1) * BLK] = block_of(k).T
+
+            @pl.when(jnp.logical_not(flip))
+            def _():
+                held[a * BLK : (a + 1) * BLK, b * BLK : (b + 1) * BLK] = block_of(k)
+
+
+def own_kernel(flags, total, out, held, done):
+    @pl.when(flags[1] == 0)
+    def _():
+        lay_out(flags[0] == 1, held, lambda k: total[k, :BLK])
+        copy = pltpu.make_async_copy(held, half_of(out, flags[3]), done)
+        copy.start()
+        copy.wait()
+
+
+def finish_own(flags, total):
+    vmem = pl.BlockSpec(memory_space=pltpu.VMEM)
+    return pl.pallas_call(
+        own_kernel,
+        out_shape=jax.ShapeDtypeStruct((SLOT, 2 * SLOT), jnp.float32),
+        in_specs=[pl.BlockSpec(memory_space=pltpu.SMEM), vmem],
+        out_specs=pl.BlockSpec(memory_space=pl.ANY),
+        scratch_shapes=[pltpu.VMEM((SLOT, SLOT), jnp.float32), pltpu.SemaphoreType.DMA],
+        compiler_params=pltpu.CompilerParams(vmem_limit_bytes=VMEM_SMALL),
+    )(flags, total)
+
+
+def finish_kernel(flags, total, mirror, partly, out, held, whole, done):
     flip = flags[0] == 1
     special = flags[1] == 1
     half = flags[3]
@@ -329,19 +372,10 @@
 
     @pl.when(jnp.logical_not(special))
     def _():
-        for a in range(SPAN):
-            for b in range(SPAN):
-                k = a * SPAN + b
-
-                @pl.when(flip)
-                def _():
-                    out[slot(half, b, a)] = total[k, :BLK].T
-                    out[slot(1 - half, b, a)] = received(k)[:BLK].T
-
-                @pl.when(jnp.logical_not(flip))
-                def _():
-                    out[slot(half, a, b)] = total[k, :BLK]
-                    out[slot(1 - half, a, b)] = received(k)[:BLK]
+        lay_out(flip, held, lambda k: received(k)[:BLK])
+        copy = pltpu.make_async_copy(held, half_of(out, 1 - half), done)
+        copy.start()
+        copy.wait()
 
     def diagonal_group(lower):
         for a in range(SPAN):
@@ -354,37 +388,50 @@
                     rows > cols, first[:BLK], jnp.where(rows < cols, second[:BLK], middle)
                 )
                 if lower:
-                    out[slot(half, a, b)] = cross
+                    whole[slot(half, a, b)] = cross
                 else:
-                    out[slot(half, b, a)] = cross.T
+                    whole[slot(half, b, a)] = cross.T
                 if a != b:
-                    out[slot(1 - half, a, b)] = jnp.zeros((BLK, BLK), jnp.float32)
+                    whole[slot(1 - half, a, b)] = jnp.zeros((BLK, BLK), jnp.float32)
         for a in range(SPAN):
             held = jnp.zeros((BLK, BLK), jnp.float32)
             for b in range(SPAN):
                 held += total[a * SPAN + b if lower else b * SPAN + a, :BLK]
             keep = rows < cols if lower else rows > cols
             strict = jnp.where(keep, held, 0.0)
-            out[slot(1 - half, a, a)] = jnp.where(rows == cols, held, strict + strict.T)
-
-    @pl.when(jnp.logical_and(special, flags[2] == 1))
+            whole[slot(1 - half, a, a)] = jnp.where(rows == cols, held, strict + strict.T)
+
+    @pl.when(special)
     def _():
-        diagonal_group(True)
-
-    @pl.when(jnp.logical_and(special, flags[2] == 0))
-    def _():
-        diagonal_group(False)
-
-
-def finish(flags, total, mirror):
+        @pl.when(flags[2] == 1)
+        def _():
+            diagonal_group(True)
+
+        @pl.when(flags[2] == 0)
+        def _():
+            diagonal_group(False)
+
+        copy = pltpu.make_async_copy(whole, out, done)
+        copy.start()
+        copy.wait()
+
+
+def finish(flags, total, mirror, partly):
     vmem = pl.BlockSpec(memory_space=pltpu.VMEM)
+    anywhere = pl.BlockSpec(memory_space=pl.ANY)
     return pl.pallas_call(
         finish_kernel,
         out_shape=jax.ShapeDtypeStruct((SLOT, 2 * SLOT), jnp.float32),
-        in_specs=[pl.BlockSpec(memory_space=pltpu.SMEM), vmem, vmem],
-        out_specs=vmem,
+        in_specs=[pl.BlockSpec(memory_space=pltpu.SMEM), vmem, vmem, anywhere],
+        out_specs=anywhere,
+        scratch_shapes=[
+            pltpu.VMEM((SLOT, SLOT), jnp.float32),
+            pltpu.VMEM((SLOT, 2 * SLOT), jnp.float32),
+            pltpu.SemaphoreType.DMA,
+        ],
+        input_output_aliases={3: 0},
         compiler_params=pltpu.CompilerParams(vmem_limit_bytes=VMEM_SMALL),
-    )(flags, total, mirror)
+    )(flags, total, mirror, partly)
 
 
 def per_device(density_matrix, basis_values, block_list, point_counts, core_density, grid_weights):
@@ -426,7 +473,8 @@
     landed = lax.all_to_all(pieces, AXES, split_axis=0, concat_axis=0, tiled=True)
     total, copy = sum_pieces(index, landed)
     returned = lax.ppermute(copy, AXES, [(target, source) for source, target in pairs])
-    return density.reshape(1, PTS), finish(flags, total, returned)
+    partly = finish_own(flags, total)
+    return density.reshape(1, PTS), finish(flags, total, returned, partly)
 
 
 def solution(mesh):

time: 225 us -> 225 us (level)
  waiting for transfers between devices: 77.8 us -> 74.7 us
  Pallas kernels: 36.8 us -> 39.3 us
    ppermute x1, waiting for transfers between devices: 27.1 us -> 24 us  [per_device(): lax.ppermute(copy, AXES, [(target, source) for source, target in pairs])]
    pallas_call x0 -> x1, Pallas kernels: none -> 3.12 us  [finish_own(): pl.pallas_call(own_kernel, out_shape=jax.ShapeDtypeStruct((SLOT, 2 * SLOT...]
  transfers between devices with their start and end apart: 4 -> 4, of which waited for: 3 -> 3; matrix products, arithmetic and copies ran while one was open for 10% -> 10% of each run, Pallas kernels for 0% -> 1%
where the time goes in v4:
time: 225 us; the launch traced here: 224 us
  waiting for transfers between devices  74.7 us (33%)
  blocking collectives  60 us (27%)
  Pallas kernels  39.3 us (17%)
  starting transfers between devices  21.8 us (10%)
  local copies, waits for them, and re-layouts  20.1 us (9%)
  other arithmetic  6.47 us (3%)
    all_to_all x1, blocking collectives, per_device(): lax.all_to_all(pieces, AXES, split_axis=0, concat_axis=0, tiled=True)  60 us
    all_to_all x1, waiting for transfers between devices, per_device(): lax.all_to_all(picked, AXES, split_axis=0, concat_axis=0, tiled=True)  31.5 us
    pallas_call x1, Pallas kernels, batch(): pl.pallas_call(batch_kernel, out_shape=(jax.ShapeDtypeStruct((LINES, BLK)...  27.8 us
    ppermute x1, waiting for transfers between devices, per_device(): lax.ppermute(copy, AXES, [(target, source) for source, target in pairs])  24 us
    all_to_all x1, waiting for transfers between devices, per_device(): lax.all_to_all(jnp.broadcast_to(block_list, (DEVICES, KB)), AXES, split_a...  19.2 us
    unnamed x8, local copies, waits for them, and re-layouts  11.4 us
    all_to_all x1, starting transfers between devices, per_device(): lax.all_to_all(jnp.broadcast_to(block_list, (DEVICES, KB)), AXES, split_a...  9.46 us
    all_to_all x1, starting transfers between devices, per_device(): lax.all_to_all(picked, AXES, split_axis=0, concat_axis=0, tiled=True)  7.47 us
  transfers between devices with their start and end apart: 4, of which 3 were waited for; matrix products, arithmetic and copies ran while one was open for 10% of the time, Pallas kernels for 1%

profile of v4, /device:TPU:96, one launch (start us, length us, event | category | flops | bytes accessed | tf_op | source)
XLA Modules:
  0.0 223.9 jit_solution(15271493049396750364)
XLA Ops:
  0.7 1.3 broadcast_select_fusion
  2.0 1.7 collective-permute-start
  3.7 1.3 broadcast_in_dim.17
  5.0 9.5 %all-to-all-start = ((s32[128,1,16]{2,1,0:T(1,128)}), s32[128,1,16]{2,1,0:T(1,128)S(1)}, u32[]{:S(2)}, u32[]{:S(2)}) async-start(s32[128,1,16]{2,1,0:T(1,128)} %broadcast_in_dim.17), calls=%async_computation | async-start | bytes 131072 | tf_op jit(solution)/shard_map/all_to_all | solution.py:455
  14.5 0.1 pad_add_fusion.flags
  14.6 19.2 %all-to-all-done = s32[128,1,16]{2,1,0:T(1,128)S(1)} async-done(((s32[128,1,16]{2,1,0:T(1,128)}), s32[128,1,16]{2,1,0:T(1,128)S(1)}, u32[]{:S(2)}, u32[]{:S(2)}) %all-to-all-start) | async-done | bytes 8224 | tf_op jit(solution)/shard_map/all_to_all | solution.py:455
  33.9 0.1 fusion.1.index
  33.9 0.0 collective-permute-done.mirror
  34.0 2.8 %shard_map.80 = s16[128,136,128]{2,1,0:T(8,128)(2,1)S(1)} custom-call(s32[4]{0:T(128)S(1)} %pad_add_fusion.flags, s32[128]{0:T(128)S(1)} %fusion.1.index, bf16[512,512]{1,0:T(8,128)(2,1)S(1)} %get-tuple-element.12.own, bf16[512,512]{1,0:T(8,128)(2,1)S(1)} %get-tuple-element.11.other, bf16[512,512]{1,0:T(8,128)(2,1)S(1)} %collective-permute-done.mirror), custom_call_target="tpu_custom_call" | custom-call | tf_op jit(solution)/shard_map/pallas_call | solution.py:112
  36.7 0.0 copy-start
  36.7 2.1 copy-done
  38.9 0.0 copy-start.1
  38.9 0.0 copy-start.2
  38.9 7.5 %all-to-all-start.1 = ((s16[128,136,128]{2,1,0:T(8,128)(2,1)}), s16[128,136,128]{2,1,0:T(8,128)(2,1)}, u32[]{:S(2)}, u32[]{:S(2)}) async-start(s16[128,136,128]{2,1,0:T(8,128)(2,1)} %copy-done), calls=%async_computation.1 | async-start | bytes 8912896 | tf_op jit(solution)/shard_map/all_to_all | solution.py:463
  47.0 0.0 copy-done.1
  47.0 0.0 copy-done.2
  47.1 8.6 %copy.20 = bf16[1,1536,2048]{1,2,0:T(8,128)(2,1)} copy(bf16[1,1536,2048]{2,1,0:T(8,128)(2,1)} %param.7) | data formatting | bytes 12582912 | tf_op args[1]
  55.7 4.9 %bitcast_convert_fusion = f8e4m3fn[1536,2048]{0,1:T(32,128)(4,1)S(1)} fusion(bf16[1,1536,2048]{1,2,0:T(8,128)(2,1)} %copy.20), kind=kLoop, calls=%fused_computation | loop fusion | flops 3145728 | bytes 9437184 | tf_op jit(solution)/shard_map/convert_element_type | solution.py:468
  60.6 7.4 %copy.22.coarse = f8e4m3fn[1536,2048]{1,0:T(32,128)(4,1)S(1)} copy(f8e4m3fn[1536,2048]{0,1:T(32,128)(4,1)S(1)} %bitcast_convert_fusion) | data formatting | bytes 6291456 | tf_op jit(solution)/shard_map/convert_element_type | solution.py:468
  68.1 31.5 %all-to-all-done.1.blocks_in = s16[128,136,128]{2,1,0:T(8,128)(2,1)} async-done(((s16[128,136,128]{2,1,0:T(8,128)(2,1)}), s16[128,136,128]{2,1,0:T(8,128)(2,1)}, u32[]{:S(2)}, u32[]{:S(2)}) %all-to-all-start.1) | async-done | bytes 4456480 | tf_op jit(solution)/shard_map/all_to_all | solution.py:463
  99.5 27.8 %shard_map.81 = (f32[12,128]{1,0:T(8,128)S(1)}, s16[128,136,128]{2,1,0:T(8,128)(2,1)S(1)}) custom-call(s32[1]{0:T(128)S(6)} %copy.28.count, s16[128,136,128]{2,1,0:T(8,128)(2,1)} %all-to-all-done.1.blocks_in, bf16[1536,2048]{1,0:T(8,128)(2,1)} %bitcast.27, f8e4m3fn[1536,2048]{1,0:T(32,128)(4,1)S(1)} %copy.22.coarse, bf16[2048,1536]{1,0:T(8,128)(2,1)} %bitcast.26, ...), custom_call_target="tpu_custom_call" | custom-call | tf_op jit(solution)/shard_map/pallas_call | solution.py:274
  127.3 60.0 %all_to_all.19.pieces = s16[128,136,128]{2,1,0:T(8,128)(2,1)S(1)} all-to-all(s16[128,136,128]{2,1,0:T(8,128)(2,1)S(1)} %get-tuple-element.7), channel_id=1, replica_groups=mesh['group'=16,'inner'=8] {'group','inner'}, dimensions={0} | all-to-all | bytes 8912896 | tf_op jit(solution)/shard_map/all_to_all | solution.py:473
  187.3 2.3 %shard_map.82 = (f32[16,136,128]{2,1,0:T(8,128)S(1)}, s16[16,136,128]{2,1,0:T(8,128)(2,1)S(1)}) custom-call(s32[128]{0:T(128)S(1)} %fusion.1.index, s16[128,136,128]{2,1,0:T(8,128)(2,1)S(1)} %all_to_all.19.pieces), custom_call_target="tpu_custom_call" | custom-call | tf_op jit(solution)/shard_map/pallas_call | solution.py:312
  189.6 3.1 %collective-permute-start.1 = (s16[16,136,128]{2,1,0:T(8,128)(2,1)S(1)}, s16[16,136,128]{2,1,0:T(8,128)(2,1)S(1)}, u32[]{:S(2)}, u32[]{:S(2)}) collective-permute-start(s16[16,136,128]{2,1,0:T(8,128)(2,1)S(1)} %get-tuple-element.9), channel_id=1, source_target_pairs={{8,0},{24,1},{40,2},{56,3},{72,4},{88,5},{104,6},{120,7},{0,8},{16... | collective-permute-start | bytes 1671176 | tf_op jit(solution)/shard_map/ppermute | solution.py:475
  192.8 0.6 copy.26
  193.4 3.1 %shard_map.83.partly = f32[512,1024]{1,0:T(8,128)} custom-call(s32[4]{0:T(128)S(1)} %pad_add_fusion.flags, f32[16,136,128]{2,1,0:T(8,128)S(1)} %get-tuple-element.8.total), custom_call_target="tpu_custom_call" | custom-call | tf_op jit(solution)/shard_map/pallas_call | solution.py:350
  196.5 24.0 %collective-permute-done.1.mirror = s16[16,136,128]{2,1,0:T(8,128)(2,1)S(1)} collective-permute-done((s16[16,136,128]{2,1,0:T(8,128)(2,1)S(1)}, s16[16,136,128]{2,1,0:T(8,128)(2,1)S(1)}, u32[]{:S(2)}, u32[]{:S(2)}) %collective-permute-start.1) | collective-permute-done | bytes 557088 | tf_op jit(solution)/shard_map/ppermute | solution.py:475
  220.5 3.3 %shard_map.84 = f32[512,1024]{1,0:T(8,128)} custom-call(s32[4]{0:T(128)S(1)} %pad_add_fusion.flags, f32[16,136,128]{2,1,0:T(8,128)S(1)} %get-tuple-element.8.total, s16[16,136,128]{2,1,0:T(8,128)(2,1)S(1)} %collective-permute-done.1.mirror, f32[512,1024]{1,0:T(8,128)} %shard_map.83.partly), custom_call_target="tpu_custom_call", output_to_operand_aliasing={{}: (3, {})} | custom-call | tf_op jit(solution)/shard_map/pallas_call | solution.py:422
  (4 shorter events, 0.1 us)
Async XLA Ops:
  2.0 32.0 %collective-permute-start = (bf16[512,512]{1,0:T(8,128)(2,1)S(1)}, bf16[512,512]{1,0:T(8,128)(2,1)S(1)}, u32[]{:S(2)}, u32[]{:S(2)}) collective-permute-start(bf16[512,512]{1,0:T(8,128)(2,1)S(1)} %get-tuple-element.10), channel_id=1, source_target_pairs={{0,8},{1,24},{2,40},{3,56},{4,72},{5,88},{6,104},{7,120},{8,0},{9,... | collective-permute-start | bytes 1572872 | tf_op jit(solution)/shard_map/ppermute | solution.py:454
  5.0 28.8 %all-to-all-start = ((s32[128,1,16]{2,1,0:T(1,128)}), s32[128,1,16]{2,1,0:T(1,128)S(1)}, u32[]{:S(2)}, u32[]{:S(2)}) async-start(s32[128,1,16]{2,1,0:T(1,128)} %broadcast_in_dim.17), calls=%async_computation | async-start | bytes 131072 | tf_op jit(solution)/shard_map/all_to_all | solution.py:455
  36.7 2.1 copy-start
  38.9 8.1 %copy-start.1 = (f32[1,1536]{1,0:T(1,128)S(1)}, f32[1,1536]{1,0:T(1,128)}, u32[]{:S(2)}) copy-start(f32[1,1536]{1,0:T(1,128)} %param.10) | copy-start | bytes 18436
  38.9 8.2 %copy-start.2 = (f32[1,1536]{1,0:T(1,128)S(1)}, f32[1,1536]{1,0:T(1,128)}, u32[]{:S(2)}) copy-start(f32[1,1536]{1,0:T(1,128)} %param.11) | copy-start | bytes 18436
  38.9 60.7 %all-to-all-start.1 = ((s16[128,136,128]{2,1,0:T(8,128)(2,1)}), s16[128,136,128]{2,1,0:T(8,128)(2,1)}, u32[]{:S(2)}, u32[]{:S(2)}) async-start(s16[128,136,128]{2,1,0:T(8,128)(2,1)} %copy-done), calls=%async_computation.1 | async-start | bytes 8912896 | tf_op jit(solution)/shard_map/all_to_all | solution.py:463
  189.6 30.8 %collective-permute-start.1 = (s16[16,136,128]{2,1,0:T(8,128)(2,1)S(1)}, s16[16,136,128]{2,1,0:T(8,128)(2,1)S(1)}, u32[]{:S(2)}, u32[]{:S(2)}) collective-permute-start(s16[16,136,128]{2,1,0:T(8,128)(2,1)S(1)} %get-tuple-element.9), channel_id=1, source_target_pairs={{8,0},{24,1},{40,2},{56,3},{72,4},{88,5},{104,6},{120,7},{0,8},{16... | collective-permute-start | bytes 1671176 | tf_op jit(solution)/shard_map/ppermute | solution.py:475
